TPU v7x, 512 devices: a whole 4x8x8 slice. The times are simulated.
512 devices in a mesh: dp: 16 (over x_hi, y), expert: 32 (over x_lo, z, core).
Axes of the slice: x: 4 (x_hi: 2, x_lo: 2; x = x_hi * 2 + x_lo), y: 8, z: 8, core: 2. Of those that a mesh axis runs over, the one named last changes fastest.
Arguments:
- projection_gradient: bfloat16 [2, 1536, 2, 12288], P(None, 'dp', None, 'expert'), may hold values from -6 to 6
- acts: bfloat16 [5120, 12288], P('dp', 'expert'), may hold values from -6 to 6
- routes: int32 [12288, 2], P('expert'), may hold values from 0 to 31, all different within a row; in each aligned block of 384 rows (0 to 383, 384 to 767, ...) at most 30 rows name the same one
- gates: bfloat16 [12288, 2], P('expert'), may hold values from 0.049804688 to 1
- tenants: int32 [12288], P('expert'), may hold values from 0 to 7
- levels: bfloat16 [32, 2, 5120, 1536], P('expert', None, 'dp'), may hold values from -8 to 7, as said below
- scales: bfloat16 [32, 2, 80, 1536], P('expert', None, 'dp'), may hold values from 0.0029907227 to 0.010986328
- adapter_first_factors: bfloat16 [32, 2, 5120, 128], P('expert', None, 'dp'), may hold values from -0.1875 to 0.1875
- adapter_second_factors: bfloat16 [32, 2, 1536, 128], P('expert', None, 'dp'), may hold values from -0.15625 to 0.15625
Outputs:
- input_grad: bfloat16 [5120, 12288], P('dp', 'expert')
- first_factor_gradient: float32 [32, 2, 5120, 128], P('expert', None, 'dp')
- second_factor_gradient: float32 [32, 2, 1536, 128], P('expert', None, 'dp')
Inputs may be any that keep to these rules, and one draw needn't show every extreme that they name: `routes`: each token names 2 different experts. Among the tokens of one index of expert (an aligned block of 384 tokens) at most 30 name any one expert, a bound that some block reaches. `levels`: whole numbers held as bfloat16.
All inputs are finite; a program needn't handle non-finite values.
Results may differ from a plain program's by a relative error of at most 0.007.
Values may be sent and summed in bfloat16 or wider, within the bound.
No kernel may reach another device: no remote copies, remote signals or barrier semaphores. Data moves between devices by JAX's collectives and lax.ppermute only.
A program may use at most 128 MiB of HBM per device.

v0:
```python
import jax
import jax.numpy as jnp
from jax import lax
from jax.sharding import PartitionSpec as P

TENANT_COUNT = 8
GROUP = 64


ADAPTER_SCALE = 2.0


def dequantize(level_block, scale_block):
    planes, rows, width = level_block.shape
    grouped = level_block.astype(jnp.float32).reshape(planes, rows // GROUP, GROUP, width)
    return (
        (grouped * scale_block.astype(jnp.float32)[:, :, None, :])
        .reshape(planes, rows, width)
        .astype(jnp.bfloat16)
    )


def tenant_select(values, onehot):
    planes, count, columns = values.shape
    shaped = values.reshape(planes, count, TENANT_COUNT, columns // TENANT_COUNT)
    return jnp.sum(shaped * onehot[None, :, :, None], axis=2)


def tenant_expand(values, onehot):
    planes, count, rank_cols = values.shape
    return (values[:, :, None, :] * onehot[None, :, :, None]).reshape(
        planes, count, TENANT_COUNT * rank_cols
    )


def on_device(
    projection_gradient,
    acts,
    routes,
    gates,
    tenants,
    levels,
    scales,
    adapter_first_factors,
    adapter_second_factors,
):
    experts = lax.axis_size("expert")
    tok_rows = acts.shape[1]
    width_rows = acts.shape[0]
    topk = routes.shape[1]
    hid_rows = projection_gradient.shape[1]
    capacity = 5 * tok_rows * topk // (4 * experts)
    slots = experts * capacity
    expert_of = routes.T.reshape(-1)
    onehot_route = (expert_of[:, None] == jnp.arange(experts, dtype=jnp.int32)[None, :]).astype(
        jnp.int32
    )
    earlier = jnp.cumsum(onehot_route, axis=0) - onehot_route
    position = expert_of * capacity + jnp.sum(earlier * onehot_route, axis=1)
    select = (jnp.arange(slots, dtype=jnp.int32)[:, None] == position[None, :]).astype(jnp.bfloat16)
    select_tok = jnp.sum(select.reshape(slots, topk, tok_rows), axis=1)
    send_x = (
        jnp.dot(acts, select_tok.T, preferred_element_type=jnp.float32)
        .astype(jnp.bfloat16)
        .reshape(width_rows, experts, capacity)
    )
    gate_flat = gates.T.reshape(-1)
    send_gate = (
        jnp.dot(select, gate_flat, preferred_element_type=jnp.float32)
        .astype(jnp.bfloat16)
        .reshape(1, experts, capacity)
    )
    send_tenant = (
        jnp.dot(select_tok, tenants.astype(jnp.bfloat16), preferred_element_type=jnp.float32)
        .astype(jnp.bfloat16)
        .reshape(1, experts, capacity)
    )
    weights = dequantize(levels[0], scales[0])
    whole = lax.all_gather(projection_gradient, "dp", axis=1, tiled=True)
    full_rows = whole.shape[1]
    send_grad = (
        jnp.dot(
            whole.reshape(2 * full_rows, topk * tok_rows),
            select.T,
            preferred_element_type=jnp.float32,
        )
        .astype(jnp.bfloat16)
        .reshape(2 * full_rows, experts, capacity)
    )
    got_grad, got_x, got_gate, got_tenant = (
        lax.all_to_all(send_grad, "expert", split_axis=1, concat_axis=1, tiled=True),
        lax.all_to_all(send_x, "expert", split_axis=1, concat_axis=1, tiled=True),
        lax.all_to_all(send_gate, "expert", split_axis=1, concat_axis=1, tiled=True),
        lax.all_to_all(send_tenant, "expert", split_axis=1, concat_axis=1, tiled=True),
    )
    full_grad = got_grad.reshape(2, full_rows, slots)
    frozen = jnp.dot(weights[0], full_grad[0], preferred_element_type=jnp.float32) + jnp.dot(
        weights[1], full_grad[1], preferred_element_type=jnp.float32
    )
    own_grad = lax.dynamic_slice_in_dim(full_grad, lax.axis_index("dp") * hid_rows, hid_rows, 1)
    inputs_x = got_x.reshape(width_rows, slots)
    gate_values = got_gate.reshape(slots).astype(jnp.float32)
    onehot_ten = (
        got_tenant.reshape(slots).astype(jnp.float32)[:, None]
        == jnp.arange(TENANT_COUNT, dtype=jnp.float32)[None, :]
    ).astype(jnp.float32)
    adapter_first = adapter_first_factors[0]
    adapter_second = adapter_second_factors[0]
    down_part = tenant_select(
        jnp.einsum("dp,jdc->jpc", inputs_x, adapter_first, preferred_element_type=jnp.float32),
        onehot_ten,
    )
    back_part = tenant_select(
        jnp.einsum("jhp,jhc->jpc", own_grad, adapter_second, preferred_element_type=jnp.float32),
        onehot_ten,
    )
    down_sum, back_sum = lax.psum((down_part, back_part), "dp")
    scale_factor = ADAPTER_SCALE * gate_values[None, :, None]
    down_scaled = tenant_expand(down_sum * scale_factor, onehot_ten).astype(jnp.bfloat16)
    back_scaled = tenant_expand(back_sum * scale_factor, onehot_ten).astype(jnp.bfloat16)
    adapter_dx = jnp.einsum(
        "jdc,jpc->dp", adapter_first, back_scaled, preferred_element_type=jnp.float32
    )
    pair_dx = (gate_values[None, :] * frozen + adapter_dx).astype(jnp.bfloat16)
    first_factor_gradient = jnp.einsum(
        "dp,jpc->jdc", inputs_x, back_scaled, preferred_element_type=jnp.float32
    )[None]
    second_factor_gradient = jnp.einsum(
        "jhp,jpc->jhc", own_grad, down_scaled, preferred_element_type=jnp.float32
    )[None]
    returned = lax.all_to_all(
        pair_dx.reshape(width_rows, experts, capacity),
        "expert",
        split_axis=1,
        concat_axis=1,
        tiled=True,
    ).reshape(width_rows, slots)
    input_grad = jnp.dot(returned, select_tok, preferred_element_type=jnp.float32).astype(
        jnp.bfloat16
    )
    return (input_grad, first_factor_gradient, second_factor_gradient)


def solution(mesh):
    return jax.shard_map(
        on_device,
        mesh=mesh,
        in_specs=(
            P(None, "dp", None, "expert"),
            P("dp", "expert"),
            P("expert", None),
            P("expert", None),
            P("expert"),
            P("expert", None, "dp", None),
            P("expert", None, "dp", None),
            P("expert", None, "dp", None),
            P("expert", None, "dp", None),
        ),
        out_specs=(P("dp", "expert"), P("expert", None, "dp", None), P("expert", None, "dp", None)),
        check_vma=False,
    )
```

profile of v0, /device:TPU:1, one launch (start us, length us, event | category | flops | bytes accessed | tf_op | source)
XLA Modules:
  0.0 524.7 jit_solution(10422574830043084562)
XLA Ops:
  7.2 0.7 all-gather.2.cloned.1.call-update
  7.9 0.7 eq.64
  8.6 0.7 reshape.170
  9.3 1.7 reduce-window.6
  11.5 0.7 convert_element_type.122
  12.2 0.7 multiply_add_fusion.1
  12.9 0.7 fusion.3
  13.8 0.7 reshape.197
  14.6 12.9 %all-to-all-start.2 = ((bf16[1,32,30]{2,0,1:T(2,128)(2,1)}), bf16[1,32,30]{2,0,1:T(2,128)(2,1)S(1)}, u32[]{:S(2)}, u32[]{:S(2)}) async-start(bf16[1,32,30]{2,0,1:T(2,128)(2,1)} %reshape.197), calls=%async_computation.2 | async-start | bytes 32768 | tf_op jit(solution)/shard_map/all_to_all | solution.py:94
  27.5 0.7 copy.76
  28.2 0.6 fusion.1
  28.8 0.7 reshape.196
  29.5 5.7 %all-to-all-done.2 = bf16[1,32,30]{2,0,1:T(2,128)(2,1)S(1)} async-done(((bf16[1,32,30]{2,0,1:T(2,128)(2,1)}), bf16[1,32,30]{2,0,1:T(2,128)(2,1)S(1)}, u32[]{:S(2)}, u32[]{:S(2)}) %all-to-all-start.2) | async-done | bytes 1952 | tf_op jit(solution)/shard_map/all_to_all | solution.py:94
  35.3 4.3 all-to-all-start
  39.6 0.5 fusion.9
  40.1 0.4 copy.60
  40.5 1.2 reshape.181
  41.7 5.7 %all-to-all-done = bf16[1,32,30]{2,0,1:T(2,128)(2,1)S(1)} async-done(((bf16[1,32,30]{2,0,1:T(2,128)(2,1)}), bf16[1,32,30]{2,0,1:T(2,128)(2,1)S(1)}, u32[]{:S(2)}, u32[]{:S(2)}) %all-to-all-start) | async-done | bytes 1952 | tf_op jit(solution)/shard_map/all_to_all | solution.py:93
  47.4 4.4 all-to-all-start.4
  51.8 71.1 %all-gather.2.cloned.1.call-done = bf16[2,1536,2,384]{3,2,1,0:T(2,128)(2,1)} async-done(((bf16[2,96,2,384]{3,2,1,0:T(2,128)(2,1)}), bf16[2,1536,2,384]{3,2,1,0:T(2,128)(2,1)}) %all-gather.2.cloned.1.call-update) | async-done | bytes 4718608 | tf_op jit(solution)/shard_map/all_gather | solution.py:79
  122.9 3.1 copy.77
  126.1 6.8 %convert_bitcast_fusion = bf16[3072,960]{0,1:T(8,128)(2,1)} fusion(bf16[3072,768]{1,0:T(8,128)(2,1)S(1)} %bitcast.124, s32[768]{0:T(1024)S(1)} %multiply_add_fusion), kind=kOutput, calls=%fused_computation | convolution fusion | flops 4533534720 | bytes 10619904 | tf_op jit(solution)/shard_map/dot_general | solution.py:82
  132.9 8.2 %reshape.175 = bf16[3072,32,30]{0,2,1:T(8,128)(2,1)} reshape(bf16[3072,960]{0,1:T(8,128)(2,1)} %convert_bitcast_fusion) | data formatting | bytes 11796480 | tf_op jit(solution)/shard_map/reshape | solution.py:88
  141.1 11.4 %all-to-all-start.1 = ((bf16[3072,32,30]{0,2,1:T(8,128)(2,1)}), bf16[3072,32,30]{0,2,1:T(8,128)(2,1)}, u32[]{:S(2)}, u32[]{:S(2)}) async-start(bf16[3072,32,30]{0,2,1:T(8,128)(2,1)} %reshape.175), calls=%async_computation.1 | async-start | bytes 12582912 | tf_op jit(solution)/shard_map/all_to_all | solution.py:91
  152.8 3.2 fusion
  156.7 0.4 convolution_bitcast_fusion.1
  157.1 1.3 copy.64
  158.4 133.3 %all-to-all-done.1 = bf16[3072,32,30]{0,2,1:T(8,128)(2,1)} async-done(((bf16[3072,32,30]{0,2,1:T(8,128)(2,1)}), bf16[3072,32,30]{0,2,1:T(8,128)(2,1)}, u32[]{:S(2)}, u32[]{:S(2)}) %all-to-all-start.1) | async-done | bytes 5898272 | tf_op jit(solution)/shard_map/all_to_all | solution.py:91
  291.8 14.1 %reshape.176 = bf16[2,1536,960]{1,0,2:T(2,128)(2,1)} reshape(bf16[3072,32,30]{0,2,1:T(8,128)(2,1)} %all-to-all-done.1) | data formatting | bytes 11796480 | tf_op jit(solution)/shard_map/reshape | solution.py:96
  305.9 1.9 constant_dynamic-slice_fusion
  307.8 1.4 copy.74
  309.2 5.1 fusion.24
  314.3 4.5 squeeze.21
  318.8 2.4 squeeze.23
  321.2 1.5 fusion.21
  322.7 2.2 multiply_reduce_fusion
  324.9 2.6 fusion.12
  327.6 1.2 fusion.7
  328.9 144.9 %all-reduce.3.cloned.1.call-done = (f32[2,960,16]{1,2,0:T(8,128)}, f32[2,960,16]{1,2,0:T(8,128)}) async-done(((f32[2,960,16]{1,2,0:T(8,128)}, f32[2,960,16]{1,2,0:T(8,128)}), (f32[2,960,16]{1,2,0:T(8,128)}, f32[2,960,16]{1,2,0:T(8,128)})) %all-reduce.3.cloned.1.call-update) | async-done | bytes 245776 | tf_op jit(solution)/shard_map/psum | solution.py:117
  473.7 1.0 broadcast_multiply_fusion
  475.4 0.4 copy.59
  475.7 1.1 reshape.179
  476.9 18.1 %all-to-all-start.3 = ((bf16[320,32,30]{0,2,1:T(8,128)(2,1)}), bf16[320,32,30]{0,2,1:T(8,128)(2,1)S(1)}, u32[]{:S(2)}, u32[]{:S(2)}) async-start(bf16[320,32,30]{0,2,1:T(8,128)(2,1)} %reshape.179), calls=%async_computation.3 | async-start | bytes 1572864 | tf_op jit(solution)/shard_map/all_to_all | solution.py:131
  495.0 0.9 convolution_bitcast_fusion.3
  496.0 0.8 multiply_convert_fusion
  496.8 1.2 convolution_bitcast_fusion.2
  498.0 18.3 %all-to-all-done.3 = bf16[320,32,30]{0,2,1:T(8,128)(2,1)S(1)} async-done(((bf16[320,32,30]{0,2,1:T(8,128)(2,1)}), bf16[320,32,30]{0,2,1:T(8,128)(2,1)S(1)}, u32[]{:S(2)}, u32[]{:S(2)}) %all-to-all-start.3) | async-done | bytes 614432 | tf_op jit(solution)/shard_map/all_to_all | solution.py:131
  516.6 1.2 convolution_convert_fusion.1
  (55 shorter events, 2.8 us)
Async XLA Ops:
  7.2 32.4 %copy-start = (bf16[320,384]{1,0:T(8,128)(2,1)S(1)}, bf16[320,384]{1,0:T(8,128)(2,1)}, u32[]{:S(2)}) copy-start(bf16[320,384]{1,0:T(8,128)(2,1)} %param.10) | copy-start | bytes 737284
  7.2 115.7 %all-gather.2.cloned.1.call-start = ((), (), s32[]{:S(2)}) async-start(), calls=%async_computation.5 | async-start | bytes 5013504 | tf_op jit(solution)/shard_map/all_gather | solution.py:79
  13.5 28.1 %copy-start.4 = (bf16[960,384]{1,0:T(8,128)(2,1)}, bf16[960,384]{1,0:T(8,128)(2,1)S(1)}, u32[]{:S(2)}) copy-start(bf16[960,384]{1,0:T(8,128)(2,1)S(1)} %fusion.3) | copy-start | bytes 2211844
  14.6 20.7 %all-to-all-start.2 = ((bf16[1,32,30]{2,0,1:T(2,128)(2,1)}), bf16[1,32,30]{2,0,1:T(2,128)(2,1)S(1)}, u32[]{:S(2)}, u32[]{:S(2)}) async-start(bf16[1,32,30]{2,0,1:T(2,128)(2,1)} %reshape.197), calls=%async_computation.2 | async-start | bytes 32768 | tf_op jit(solution)/shard_map/all_to_all | solution.py:94
  35.3 12.1 %all-to-all-start = ((bf16[1,32,30]{2,0,1:T(2,128)(2,1)}), bf16[1,32,30]{2,0,1:T(2,128)(2,1)S(1)}, u32[]{:S(2)}, u32[]{:S(2)}) async-start(bf16[1,32,30]{2,0,1:T(2,128)(2,1)} %reshape.196), calls=%async_computation | async-start | bytes 32768 | tf_op jit(solution)/shard_map/all_to_all | solution.py:93
  47.4 93.6 %all-to-all-start.4 = ((bf16[320,32,30]{0,2,1:T(8,128)(2,1)}), bf16[320,32,30]{0,2,1:T(8,128)(2,1)S(1)}, u32[]{:S(2)}, u32[]{:S(2)}) async-start(bf16[320,32,30]{0,2,1:T(8,128)(2,1)} %reshape.181), calls=%async_computation.4 | async-start | bytes 1572864 | tf_op jit(solution)/shard_map/all_to_all | solution.py:92
  141.1 11.6 %copy-start.13 = (bf16[1,2,5,1536]{3,1,2,0:T(2,128)(2,1)S(1)}, bf16[1,2,5,1536]{3,1,2,0:T(2,128)(2,1)}, u32[]{:S(2)}) copy-start(bf16[1,2,5,1536]{3,1,2,0:T(2,128)(2,1)} %param.15) | copy-start | bytes 92164
  141.1 150.7 %all-to-all-start.1 = ((bf16[3072,32,30]{0,2,1:T(8,128)(2,1)}), bf16[3072,32,30]{0,2,1:T(8,128)(2,1)}, u32[]{:S(2)}, u32[]{:S(2)}) async-start(bf16[3072,32,30]{0,2,1:T(8,128)(2,1)} %reshape.175), calls=%async_computation.1 | async-start | bytes 12582912 | tf_op jit(solution)/shard_map/all_to_all | solution.py:91
  152.4 321.3 %all-reduce.3.cloned.1.call-start = ((), (), s32[]{:S(2)}) async-start(), calls=%async_computation.6 | async-start | bytes 524288 | tf_op jit(solution)/shard_map/psum | solution.py:117
  152.7 4.0 copy-start.10
  156.3 318.4 %copy-start.11 = (f32[960,8]{0,1:T(8,128)}, f32[960,8]{0,1:T(8,128)S(1)}, u32[]{:S(2)}) copy-start(f32[960,8]{0,1:T(8,128)S(1)} %fusion.23) | copy-start | bytes 92164
  156.7 149.2 %copy-start.2 = (bf16[320,960]{0,1:T(8,128)(2,1)}, bf16[320,960]{0,1:T(8,128)(2,1)S(1)}, u32[]{:S(2)}) copy-start(bf16[320,960]{0,1:T(8,128)(2,1)S(1)} %reshape.182) | copy-start | bytes 1843204
  318.8 2.4 copy-start.12
  321.2 3.7 copy-start.8
  324.9 2.6 copy-start.7
  324.9 2.7 copy-start.9
  475.0 20.0 %copy-start.6 = (bf16[2,96,960]{2,1,0:T(8,128)(2,1)S(1)}, bf16[2,96,960]{2,1,0:T(8,128)(2,1)}, u32[]{:S(2)}) copy-start(bf16[2,96,960]{2,1,0:T(8,128)(2,1)} %copy.74) | copy-start | bytes 1105924
  475.3 21.5 %copy-start.3 = (bf16[320,960]{0,1:T(8,128)(2,1)S(1)}, bf16[320,960]{0,1:T(8,128)(2,1)}, u32[]{:S(2)}) copy-start(bf16[320,960]{0,1:T(8,128)(2,1)} %copy-done.2) | copy-start | bytes 1843204
  476.9 39.7 %copy-start.5 = (bf16[960,384]{1,0:T(8,128)(2,1)S(1)}, bf16[960,384]{1,0:T(8,128)(2,1)}, u32[]{:S(2)}) copy-start(bf16[960,384]{1,0:T(8,128)(2,1)} %copy-done.4) | copy-start | bytes 2211844
  476.9 39.4 %all-to-all-start.3 = ((bf16[320,32,30]{0,2,1:T(8,128)(2,1)}), bf16[320,32,30]{0,2,1:T(8,128)(2,1)S(1)}, u32[]{:S(2)}, u32[]{:S(2)}) async-start(bf16[320,32,30]{0,2,1:T(8,128)(2,1)} %reshape.179), calls=%async_computation.3 | async-start | bytes 1572864 | tf_op jit(solution)/shard_map/all_to_all | solution.py:131
  495.0 22.8 %copy-start.1 = (bf16[320,384]{1,0:T(8,128)(2,1)S(1)}, bf16[320,384]{1,0:T(8,128)(2,1)}, u32[]{:S(2)}) copy-start(bf16[320,384]{1,0:T(8,128)(2,1)} %param.10) | copy-start | bytes 737284
Sparse Core Ops, SparseCore 0:
  11.2 111.6 all-gather.1
  325.0 148.6 all-reduce.2
where the time goes:
time: 526 us; the launch traced here: 525 us
  waiting for transfers between devices  380 us (72%)
  starting transfers between devices  51.3 us (10%)
  local copies, waits for them, and re-layouts  50.1 us (10%)
  matrix products  17.5 us (3%)
  between operations  14.4 us (3%)
  other arithmetic  11.5 us (2%)
    psum x1, waiting for transfers between devices, on_device(): down_sum, back_sum = lax.psum((down_part, back_part), 'dp')  145 us
    all_to_all x1, waiting for transfers between devices, on_device(): lax.all_to_all(send_grad, 'expert', split_axis=1, concat_axis=1, tiled=True)  133 us
    all_gather x1, waiting for transfers between devices, on_device(): whole = lax.all_gather(projection_gradient, 'dp', axis=1, tiled=True)  71.1 us
    all_to_all x1, waiting for transfers between devices, on_device(): lax.all_to_all(pair_dx.reshape(width_rows, experts, capacity), 'expert',...  18.3 us
    all_to_all x1, starting transfers between devices, on_device(): lax.all_to_all(pair_dx.reshape(width_rows, experts, capacity), 'expert',...  18.1 us
    reshape x1, local copies, waits for them, and re-layouts, on_device(): full_grad = got_grad.reshape(2, full_rows, slots)  14.1 us
    all_to_all x1, starting transfers between devices, on_device(): lax.all_to_all(send_tenant, 'expert', split_axis=1, concat_axis=1, tiled=...  12.9 us
    all_to_all x1, starting transfers between devices, on_device(): lax.all_to_all(send_grad, 'expert', split_axis=1, concat_axis=1, tiled=True)  11.4 us
  transfers between devices with their start and end apart: 7, of which 6 were waited for; matrix products, arithmetic and copies ran while one was open for 8% of the time, Pallas kernels for 0%

commit v1 on v0

v1 whole, which is shorter than its diff:
```python
import functools

import jax
import jax.numpy as jnp
from jax import lax
from jax.experimental import pallas as pl
from jax.experimental.pallas import tpu as pltpu
from jax.sharding import Mesh
from jax.sharding import PartitionSpec as P

TENANT_COUNT = 8
GROUP = 64
ADAPTER_SCALE = 2.0
BF = jnp.bfloat16
F32 = jnp.float32


def dot(a, b, dims):
    return lax.dot_general(a, b, (dims, ((), ())), preferred_element_type=F32)


def dequantize(level_block, scale_block):
    planes, rows, width = level_block.shape
    grouped = level_block.astype(F32).reshape(planes, rows // GROUP, GROUP, width)
    return (
        (grouped * scale_block.astype(F32)[:, :, None, :]).reshape(planes, rows, width).astype(BF)
    )


def pair_kernel(
    hid, rank, z_ref, second_ref, gate_ref, row_ref, weight_ref, first_ref, dx_ref, back_ref, wide_ref
):
    depth, cols = second_ref.shape

    @pl.when(pl.program_id(0) == 0)
    def _():
        row = lax.broadcasted_iota(jnp.int32, (depth, cols), 0)
        plane = (row // hid) % 2
        second = second_ref[...].astype(F32)
        wide_ref[:, :cols] = jnp.where(plane == 0, second, 0.0).astype(BF)
        wide_ref[:, cols:] = jnp.where(plane == 1, second, 0.0).astype(BF)

    z = z_ref[...]
    tile = z.shape[1]
    gate = gate_ref[:, 0:1].astype(F32)
    tenant = gate_ref[:, 1:2].astype(F32)
    lane = lax.broadcasted_iota(jnp.int32, (tile, 2 * cols), 1)
    mine = ((lane % cols) // rank).astype(F32) == tenant
    back = dot(z, wide_ref[...], ((0,), (0,)))
    back_scaled = jnp.where(mine, back * (ADAPTER_SCALE * gate), 0.0).astype(BF)
    frozen = dot(z, weight_ref[...], ((0,), (0,)))
    out = gate * frozen + dot(back_scaled, first_ref[...], ((1,), (0,)))
    half = out.shape[1] // 2
    dx_ref[0] = out[:, :half].astype(BF)
    dx_ref[1] = out[:, half:].astype(BF)
    across = dot(wide_ref[...], z, ((0,), (0,)))
    tenant_row = row_ref[1:2, :].astype(F32)
    for plane in range(2):
        total = jnp.zeros((rank, tile), F32)
        for t in range(cols // rank):
            start = plane * cols + t * rank
            total += jnp.where(tenant_row == float(t), across[start : start + rank], 0.0)
        back_ref[plane * rank : (plane + 1) * rank, :] = total


def pair_call(gathered, slot_rows, slot_cols, weights, first, hid, rank, slots):
    depth, wide = gathered.shape
    cols = wide - slots
    width = weights.shape[1]
    tile = 256 if slots % 256 == 0 else slots
    return pl.pallas_call(
        functools.partial(pair_kernel, hid, rank),
        grid=(slots // tile,),
        in_specs=[
            pl.BlockSpec((depth, tile), lambda i: (0, i)),
            pl.BlockSpec((depth, cols), lambda i: (0, slots // cols)),
            pl.BlockSpec((tile, slot_rows.shape[1]), lambda i: (i, 0)),
            pl.BlockSpec((slot_cols.shape[0], tile), lambda i: (0, i)),
            pl.BlockSpec((depth, width), lambda i: (0, 0)),
            pl.BlockSpec((2 * cols, width), lambda i: (0, 0)),
        ],
        out_specs=[
            pl.BlockSpec((2, tile, width // 2), lambda i: (0, i, 0)),
            pl.BlockSpec((2 * rank, tile), lambda i: (0, i)),
        ],
        out_shape=[
            jax.ShapeDtypeStruct((2, slots, width // 2), BF),
            jax.ShapeDtypeStruct((2 * rank, slots), F32),
        ],
        scratch_shapes=[pltpu.VMEM((depth, 2 * cols), BF)],
        compiler_params=pltpu.CompilerParams(vmem_limit_bytes=40 * 1024 * 1024),
        cost_estimate=pl.CostEstimate(
            flops=2 * slots * depth * (width + 4 * cols),
            bytes_accessed=2 * depth * (wide + width) + 2 * slots * width,
            transcendentals=0,
        ),
    )(gathered, gathered, slot_rows, slot_cols, weights, first)


def on_device(
    projection_gradient,
    acts,
    routes,
    gates,
    tenants,
    levels,
    scales,
    adapter_first_factors,
    adapter_second_factors,
):
    experts = lax.axis_size("expert")
    ring = lax.axis_size("y")
    half = lax.axis_index("xh")
    planes, hid, topk, toks = projection_gradient.shape
    width_rows = acts.shape[0]
    rank = adapter_first_factors.shape[3] // TENANT_COUNT
    cols = TENANT_COUNT * rank
    capacity = 5 * toks * topk // (4 * experts)
    room = -(-capacity // 16) * 16
    slots = experts * room
    own = planes * hid

    expert_ids = lax.broadcasted_iota(jnp.int32, (experts, toks), 0)
    named = [routes[:, k][None, :] == expert_ids for k in range(topk)]
    member = functools.reduce(jnp.logical_or, named).astype(BF)
    before = (
        lax.broadcasted_iota(jnp.int32, (toks, toks), 0)
        < lax.broadcasted_iota(jnp.int32, (toks, toks), 1)
    ).astype(BF)
    place = dot(member, before, ((1,), (0,))).astype(jnp.int32) + expert_ids * room
    position = [jnp.sum(jnp.where(m, place, 0), axis=0) for m in named]
    slot_ids = lax.broadcasted_iota(jnp.int32, (slots, toks), 0)
    chosen = [slot_ids == p[None, :] for p in position]
    select = jnp.concatenate([c.astype(BF) for c in chosen], axis=1)
    select_tok = functools.reduce(jnp.logical_or, chosen).astype(BF)

    spare = -(-(own + 2) // 128) * 128 - own - 2
    sent = jnp.concatenate(
        [
            projection_gradient.reshape(own, topk * toks),
            gates.T.reshape(1, topk * toks),
            jnp.tile(tenants.astype(BF)[None, :], (1, topk)),
            jnp.zeros((spare, topk * toks), BF),
        ],
        axis=0,
    )
    send_z = dot(select, sent, ((1,), (1,))).astype(BF).reshape(experts, room, -1)
    got_z = lax.all_to_all(send_z, "expert", 0, 0, tiled=True).reshape(slots, -1)
    across_z = got_z.T
    own_z = across_z[:own]
    slot_rows = got_z[:, own : own + 2]
    slot_cols = across_z[own : own + 2]

    adapter_first = adapter_first_factors[0]
    adapter_second = adapter_second_factors[0].reshape(own, cols)
    payload = jnp.concatenate([own_z, adapter_second], axis=1)
    gathered = lax.all_gather(payload, "y", axis=0, tiled=True)

    weights = dequantize(levels[0], scales[0])
    mid = weights.shape[2] // 2
    low, high = weights[:, :, :mid], weights[:, :, mid:]
    swap = [(0, 1), (1, 0)]
    got_w = lax.ppermute(jnp.where(half == 0, high, low), "xh", swap)
    kept_w = jnp.where(half == 0, low, high)
    got_first = lax.ppermute(adapter_first, "xh", swap)

    def both(kept, got):
        return jnp.stack([jnp.where(half == 0, kept, got), jnp.where(half == 0, got, kept)])

    pair_w = both(kept_w, got_w)
    pair_w = (
        pair_w.reshape(2, planes, width_rows, ring, hid)
        .transpose(3, 1, 4, 0, 2)
        .reshape(ring * own, 2 * width_rows)
    )
    pair_first = both(adapter_first, got_first).transpose(1, 3, 0, 2)
    pair_first = pair_first.reshape(planes * cols, 2 * width_rows)

    send_x = dot(select_tok, acts, ((1,), (1,))).astype(BF).reshape(experts, room, width_rows)
    got_x = lax.all_to_all(send_x, "expert", 0, 0, tiled=True).reshape(slots, width_rows)
    tenant_row = slot_cols[1].astype(F32)
    one = tenant_row[None, :] == jnp.arange(TENANT_COUNT, dtype=F32)[:, None]
    down = lax.dot_general(
        adapter_first, got_x, (((1,), (1,)), ((), ())), preferred_element_type=F32
    ).reshape(planes, TENANT_COUNT, rank, slots)
    down = jnp.sum(jnp.where(one[None, :, None, :], down, 0.0), axis=1).reshape(
        planes * rank, slots
    )
    step = 1
    while step < ring:
        down = down + lax.ppermute(down, "y", [(i, i ^ step) for i in range(ring)])
        step *= 2

    pair_dx, back = pair_call(
        gathered, slot_rows, slot_cols, pair_w, pair_first, hid, rank, slots
    )
    returned = lax.all_to_all(
        pair_dx.reshape(2 * experts, room, width_rows), ("xh", "expert"), 0, 0, tiled=True
    ).reshape(2, slots, width_rows)
    input_grad = dot(returned[0], select_tok, ((0,), (0,))) + dot(
        returned[1], select_tok, ((0,), (0,))
    )

    ranks = jnp.concatenate([down, back], axis=0)
    ranks = ranks + lax.ppermute(ranks, "xh", swap)
    scaled = (ranks * (ADAPTER_SCALE * slot_cols[0].astype(F32))[None, :]).astype(BF)
    spread = jnp.where(
        one[None, :, None, :], scaled.reshape(2 * planes, 1, rank, slots), jnp.zeros((), BF)
    ).reshape(2, planes, cols, slots)
    second_grad = jnp.stack(
        [
            dot(own_z[j * hid : (j + 1) * hid], spread[0, j], ((1,), (1,)))
            for j in range(planes)
        ]
    )
    first_grad = jnp.stack([dot(got_x, spread[1, j].T, ((0,), (0,))) for j in range(planes)])
    return input_grad.astype(BF), first_grad[None], second_grad[None]


def solution(mesh):
    groups, experts = mesh.devices.shape
    split = Mesh(mesh.devices.reshape(2, groups // 2, experts), ("xh", "y", "expert"))
    dp = ("xh", "y")
    factors = P("expert", None, dp, None)
    return jax.shard_map(
        on_device,
        mesh=split,
        in_specs=(
            P(None, dp, None, "expert"),
            P(dp, "expert"),
            P("expert", None),
            P("expert", None),
            P("expert"),
            factors,
            factors,
            factors,
            factors,
        ),
        out_specs=(P(dp, "expert"), factors, factors),
        check_vma=False,
    )
```

time: 526 us -> 182 us (0.35)
  the two profiles are of different devices: /device:TPU:1 before, /device:TPU:62 now
where the time goes in v1:
time: 182 us; the launch traced here: 181 us
  waiting for transfers between devices  49.7 us (27%)
  starting transfers between devices  36.3 us (20%)
  blocking collectives  29.1 us (16%)
  local copies, waits for them, and re-layouts  23.4 us (13%)
  between operations  14.4 us (8%)
  other arithmetic  13.2 us (7%)
  matrix products  8.47 us (5%)
  Pallas kernels  6.67 us (4%)
    all_to_all x1, blocking collectives, on_device(): lax.all_to_all(send_z, 'expert', 0, 0, tiled=True).reshape(slots, -1)  29.1 us
    ppermute x1, waiting for transfers between devices, on_device(): got_first = lax.ppermute(adapter_first, 'xh', swap)  22.1 us
    ppermute x3, waiting for transfers between devices, on_device(): down = down + lax.ppermute(down, 'y', [(i, i ^ step) for i in range(ring)])  19 us
    ppermute x3, starting transfers between devices, on_device(): down = down + lax.ppermute(down, 'y', [(i, i ^ step) for i in range(ring)])  12 us
    ppermute x1, waiting for transfers between devices, on_device(): ranks = ranks + lax.ppermute(ranks, 'xh', swap)  8.42 us
    all_to_all x1, starting transfers between devices, on_device(): lax.all_to_all(pair_dx.reshape(2 * experts, room, width_rows), ('xh', 'ex...  7.96 us
    dot_general x9, matrix products, dot(): return lax.dot_general(a, b, (dims, ((), ())), preferred_element_type=F32)  6.83 us
    pallas_call x1, Pallas kernels, pair_call(): pl.pallas_call(functools.partial(pair_kernel, hid, rank), grid=(slots //...  6.67 us
  transfers between devices with their start and end apart: 9, of which 5 were waited for; matrix products, arithmetic and copies ran while one was open for 19% of the time, Pallas kernels for 4%

profile of v1, /device:TPU:62, one launch (start us, length us, event | category | flops | bytes accessed | tf_op | source)
XLA Modules:
  0.0 181.2 jit_solution(11777131282056408809)
XLA Ops:
  7.2 0.8 slice_reduce_fusion.1
  8.0 0.7 convert_element_type.51
  8.7 0.7 copy.40
  9.4 1.0 copy.39
  10.6 0.5 iota_compare_fusion
  11.2 0.7 fusion.5
  11.9 29.1 %all_to_all.15 = bf16[32,32,256]{2,1,0:T(8,128)(2,1)S(1)} all-to-all(bf16[32,32,256]{2,1,0:T(8,128)(2,1)S(1)} %bitcast.105), channel_id=1, replica_groups=mesh['xh'=2,'y'=8,'expert'=32] {'expert'}, dimensions={0} | all-to-all | bytes 1048576 | tf_op jit(solution)/shard_map/all_to_all | solution.py:148
  41.3 1.0 pad_maximum_fusion
  42.3 1.9 %fusion = bf16[2,320,1536]{2,1,0:T(8,128)(2,1)S(1)} fusion(bf16[1,2,320,1536]{3,2,1,0:T(8,128)(2,1)} %param.14, f32[2,5,1536]{2,1,0:T(8,128)S(1)} %copy.27), kind=kLoop, calls=%fused_computation.1 | loop fusion | flops 2949120 | bytes 3993600 | tf_op jit(solution)/shard_map/convert_element_type | solution.py:26
  44.2 1.1 broadcast_select_fusion.3
  45.3 3.3 %collective-permute-start = (bf16[2,320,768]{2,1,0:T(8,128)(2,1)}, bf16[2,320,768]{2,1,0:T(8,128)(2,1)}, u32[]{:S(2)}, u32[]{:S(2)}) collective-permute-start(bf16[2,320,768]{2,1,0:T(8,128)(2,1)} %broadcast_select_fusion.3), channel_id=1, source_target_pairs={{0,256},{256,0},{1,257},{257,1},{2,258},{258,2},{3,259},{259,3},{4... | collective-permute-start | bytes 2949128 | tf_op jit(solution)/shard_map/ppermute | solution.py:163
  48.6 4.0 %collective-permute-start.1 = (bf16[2,320,128]{2,1,0:T(8,128)(2,1)}, bf16[2,320,128]{2,1,0:T(8,128)(2,1)}, u32[]{:S(2)}, u32[]{:S(2)}) collective-permute-start(bf16[2,320,128]{2,1,0:T(8,128)(2,1)} %bitcast), channel_id=1, source_target_pairs={{0,256},{256,0},{1,257},{257,1},{2,258},{258,2},{3,259},{259,3},{4... | collective-permute-start | bytes 491528 | tf_op jit(solution)/shard_map/ppermute | solution.py:165
  52.7 0.6 convolution_convert_fusion
  53.3 1.2 copy.33
  54.5 5.8 %all-to-all-start.2 = ((bf16[32,32,320]{2,1,0:T(8,128)(2,1)}), bf16[32,32,320]{2,1,0:T(8,128)(2,1)}, u32[]{:S(2)}, u32[]{:S(2)}) async-start(bf16[32,32,320]{2,1,0:T(8,128)(2,1)} %bitcast.93), calls=%async_computation.2 | async-start | bytes 1572864 | tf_op jit(solution)/shard_map/all_to_all | solution.py:180
  60.3 22.1 %collective-permute-done.1 = bf16[2,320,128]{2,1,0:T(8,128)(2,1)} collective-permute-done((bf16[2,320,128]{2,1,0:T(8,128)(2,1)}, bf16[2,320,128]{2,1,0:T(8,128)(2,1)}, u32[]{:S(2)}, u32[]{:S(2)}) %collective-permute-start.1) | collective-permute-done | bytes 163872 | tf_op jit(solution)/shard_map/ppermute | solution.py:165
  82.5 1.0 select_bitcast_fusion.1
  83.5 1.1 copy.36
  84.6 1.3 reshape.115.first_ref
  85.9 2.7 %broadcast_select_fusion.2 = (bf16[2,320,768]{2,1,0:T(8,128)(2,1)}, bf16[2,320,768]{2,1,0:T(8,128)(2,1)}) fusion(bf16[2,320,768]{2,1,0:T(8,128)(2,1)} %collective-permute-done, pred[]{:T(512)S(6)} %eq.75, bf16[2,320,1536]{2,1,0:T(8,128)(2,1)S(1)} %fusion), kind=kLoop, calls=%fused_computation.22 | loop fusion | flops 1474560 | bytes 4915201 | tf_op jit(solution)/shard_map/jit(_where)/select_n | solution.py:168
  88.6 1.7 copy.29
  90.3 2.3 %copy.28 = bf16[2,320,768]{1,2,0:T(8,128)(2,1)} copy(bf16[2,320,768]{2,1,0:T(8,128)(2,1)} %get-tuple-element.11) | data formatting | bytes 1966080 | tf_op jit(solution)/shard_map/jit(_where)/select_n | solution.py:168
  92.6 1.7 maximum_bitcast_fusion
  94.4 3.9 %copy.30 = bf16[8,2,96,2,320]{4,3,2,1,0:T(2,128)(2,1)} copy(bf16[8,2,96,2,320]{4,2,0,1,3:T(8,128)(2,1)S(1)} %maximum_bitcast_fusion) | data formatting | bytes 3932160 | tf_op jit(solution)/shard_map/transpose | solution.py:173
  98.2 4.9 %reshape.104.weight_ref = bf16[1536,640]{1,0:T(8,128)(2,1)S(1)} reshape(bf16[8,2,96,2,320]{4,3,2,1,0:T(2,128)(2,1)} %copy.30) | data formatting | bytes 3932160 | tf_op jit(solution)/shard_map/reshape | solution.py:174
  103.3 0.7 slice.76.row_ref
  104.0 0.7 slice_convert_fusion.1
  104.8 2.0 %copy-done.2 = bf16[1536,1152]{1,0:T(8,128)(2,1)S(1)} copy-done((bf16[1536,1152]{1,0:T(8,128)(2,1)S(1)}, bf16[1536,1152]{1,0:T(8,128)(2,1)}, u32[]{:S(2)}) %copy-start.2) | copy-done | bytes 3538968
  106.8 6.7 %shard_map.112 = (bf16[2,1024,320]{2,1,0:T(8,128)(2,1)S(1)}, f32[32,1024]{1,0:T(8,128)S(1)}) custom-call(bf16[1536,1152]{1,0:T(8,128)(2,1)S(1)} %copy-done.2, bf16[1536,1152]{1,0:T(8,128)(2,1)S(1)} %copy-done.2, bf16[1024,2]{1,0:T(8,128)(2,1)S(1)} %slice.75.gate_ref, bf16[2,1024]{1,0:T(2,128)(2,1)S(1)} %slice.76.row_ref, ...), custom_call_target="tpu_custom_call" | custom-call | flops 3623878656 | bytes 6815744 | tf_op jit(solution)/shard_map/pallas_call | solution.py:71
  113.4 1.2 copy-done.1
  114.6 8.0 %all-to-all-start.1 = ((bf16[64,32,320]{2,1,0:T(8,128)(2,1)}), bf16[64,32,320]{2,1,0:T(8,128)(2,1)S(1)}, u32[]{:S(2)}, u32[]{:S(2)}) async-start(bf16[64,32,320]{2,1,0:T(8,128)(2,1)} %bitcast.86), calls=%async_computation.1 | async-start | bytes 3145728 | tf_op jit(solution)/shard_map/all_to_all | solution.py:197
  122.6 1.6 fusion.31
  124.3 3.4 %collective-permute-start.2 = (f32[32,1024]{1,0:T(8,128)S(1)}, f32[32,1024]{1,0:T(8,128)S(1)}, u32[]{:S(2)}, u32[]{:S(2)}) collective-permute-start(f32[32,1024]{1,0:T(8,128)S(1)} %bitcast.102), channel_id=1, source_target_pairs={{0,32},{32,0},{64,96},{96,64},{128,160},{160,128},{192,224},{224,1... | collective-permute-start | bytes 393224 | tf_op jit(solution)/shard_map/ppermute | solution.py:191
  127.7 4.2 %collective-permute-done.2 = f32[32,1024]{1,0:T(8,128)S(1)} collective-permute-done((f32[32,1024]{1,0:T(8,128)S(1)}, f32[32,1024]{1,0:T(8,128)S(1)}, u32[]{:S(2)}, u32[]{:S(2)}) %collective-permute-start.2) | collective-permute-done | bytes 131104 | tf_op jit(solution)/shard_map/ppermute | solution.py:191
  131.9 4.0 %collective-permute-start.3 = (f32[32,1024]{1,0:T(8,128)S(1)}, f32[32,1024]{1,0:T(8,128)S(1)}, u32[]{:S(2)}, u32[]{:S(2)}) collective-permute-start(f32[32,1024]{1,0:T(8,128)S(1)} %bitcast_add_fusion), channel_id=1, source_target_pairs={{0,64},{32,96},{64,0},{96,32},{128,192},{160,224},{192,128},{224,1... | collective-permute-start | bytes 393224 | tf_op jit(solution)/shard_map/ppermute | solution.py:191
  136.0 6.3 %collective-permute-done.3 = f32[32,1024]{1,0:T(8,128)S(1)} collective-permute-done((f32[32,1024]{1,0:T(8,128)S(1)}, f32[32,1024]{1,0:T(8,128)S(1)}, u32[]{:S(2)}, u32[]{:S(2)}) %collective-permute-start.3) | collective-permute-done | bytes 131104 | tf_op jit(solution)/shard_map/ppermute | solution.py:191
  142.3 4.6 %collective-permute-start.4 = (f32[32,1024]{1,0:T(8,128)S(1)}, f32[32,1024]{1,0:T(8,128)S(1)}, u32[]{:S(2)}, u32[]{:S(2)}) collective-permute-start(f32[32,1024]{1,0:T(8,128)S(1)} %add.21), channel_id=1, source_target_pairs={{0,128},{32,160},{64,192},{96,224},{128,0},{160,32},{192,64},{224,... | collective-permute-start | bytes 393224 | tf_op jit(solution)/shard_map/ppermute | solution.py:191
  146.9 8.6 %collective-permute-done.4 = f32[32,1024]{1,0:T(8,128)S(1)} collective-permute-done((f32[32,1024]{1,0:T(8,128)S(1)}, f32[32,1024]{1,0:T(8,128)S(1)}, u32[]{:S(2)}, u32[]{:S(2)}) %collective-permute-start.4) | collective-permute-done | bytes 131104 | tf_op jit(solution)/shard_map/ppermute | solution.py:191
  155.5 3.2 %collective-permute-start.5 = (f32[64,1024]{1,0:T(8,128)S(1)}, f32[64,1024]{1,0:T(8,128)S(1)}, u32[]{:S(2)}, u32[]{:S(2)}) collective-permute-start(f32[64,1024]{1,0:T(8,128)S(1)} %pad_maximum_fusion.1), channel_id=1, source_target_pairs={{0,256},{256,0},{1,257},{257,1},{2,258},{258,2},{3,259},{259,3},{4... | collective-permute-start | bytes 786440 | tf_op jit(solution)/shard_map/ppermute | solution.py:205
  158.7 8.4 %collective-permute-done.5 = f32[64,1024]{1,0:T(8,128)S(1)} collective-permute-done((f32[64,1024]{1,0:T(8,128)S(1)}, f32[64,1024]{1,0:T(8,128)S(1)}, u32[]{:S(2)}, u32[]{:S(2)}) %collective-permute-start.5) | collective-permute-done | bytes 262176 | tf_op jit(solution)/shard_map/ppermute | solution.py:205
  167.5 0.2 convolution_bitcast_fusion.2
  167.7 0.2 convolution_bitcast_fusion.3
  167.9 0.7 maximum_bitcast_fusion.3
  168.6 1.5 convolution_bitcast_fusion
  170.1 1.5 convolution_bitcast_fusion.1
  171.6 0.7 maximum_bitcast_fusion.2
  172.5 0.6 fusion.24
  173.1 1.3 fusion.8
  (42 shorter events, 1.5 us)
Async XLA Ops:
  7.2 45.5 %copy-start = (bf16[320,384]{1,0:T(8,128)(2,1)S(1)}, bf16[320,384]{1,0:T(8,128)(2,1)}, u32[]{:S(2)}) copy-start(bf16[320,384]{1,0:T(8,128)(2,1)} %param.10) | copy-start | bytes 737284
  7.2 97.6 %all-gather.2.cloned.1.call-start = ((), (), s32[]{:S(2)}) async-start(), calls=%async_computation.3 | async-start | bytes 3981312 | tf_op jit(solution)/shard_map/all_gather | solution.py:157
  11.9 29.3 %copy-start.5 = (bf16[1,2,96,128]{3,2,1,0:T(8,128)(2,1)S(1)}, bf16[1,2,96,128]{3,2,1,0:T(8,128)(2,1)}, u32[]{:S(2)}) copy-start(bf16[1,2,96,128]{3,2,1,0:T(8,128)(2,1)} %param.17) | copy-start | bytes 147460
  41.0 1.3 copy-start.6
  41.2 1.1 copy-start.3
  45.3 40.6 %collective-permute-start = (bf16[2,320,768]{2,1,0:T(8,128)(2,1)}, bf16[2,320,768]{2,1,0:T(8,128)(2,1)}, u32[]{:S(2)}, u32[]{:S(2)}) collective-permute-start(bf16[2,320,768]{2,1,0:T(8,128)(2,1)} %broadcast_select_fusion.3), channel_id=1, source_target_pairs={{0,256},{256,0},{1,257},{257,1},{2,258},{258,2},{3,259},{259,3},{4... | collective-permute-start | bytes 2949128 | tf_op jit(solution)/shard_map/ppermute | solution.py:163
  48.6 33.9 %collective-permute-start.1 = (bf16[2,320,128]{2,1,0:T(8,128)(2,1)}, bf16[2,320,128]{2,1,0:T(8,128)(2,1)}, u32[]{:S(2)}, u32[]{:S(2)}) collective-permute-start(bf16[2,320,128]{2,1,0:T(8,128)(2,1)} %bitcast), channel_id=1, source_target_pairs={{0,256},{256,0},{1,257},{257,1},{2,258},{258,2},{3,259},{259,3},{4... | collective-permute-start | bytes 491528 | tf_op jit(solution)/shard_map/ppermute | solution.py:165
  54.5 60.1 %all-to-all-start.2 = ((bf16[32,32,320]{2,1,0:T(8,128)(2,1)}), bf16[32,32,320]{2,1,0:T(8,128)(2,1)}, u32[]{:S(2)}, u32[]{:S(2)}) async-start(bf16[32,32,320]{2,1,0:T(8,128)(2,1)} %bitcast.93), calls=%async_computation.2 | async-start | bytes 1572864 | tf_op jit(solution)/shard_map/all_to_all | solution.py:180
  104.7 2.0 %copy-start.2 = (bf16[1536,1152]{1,0:T(8,128)(2,1)S(1)}, bf16[1536,1152]{1,0:T(8,128)(2,1)}, u32[]{:S(2)}) copy-start(bf16[1536,1152]{1,0:T(8,128)(2,1)} %all-gather.2.cloned.1.call-done.z_ref.second_ref) | copy-start | bytes 10616836
  113.4 1.2 copy-start.1
  114.6 57.8 %all-to-all-start.1 = ((bf16[64,32,320]{2,1,0:T(8,128)(2,1)}), bf16[64,32,320]{2,1,0:T(8,128)(2,1)S(1)}, u32[]{:S(2)}, u32[]{:S(2)}) async-start(bf16[64,32,320]{2,1,0:T(8,128)(2,1)} %bitcast.86), calls=%async_computation.1 | async-start | bytes 3145728 | tf_op jit(solution)/shard_map/all_to_all | solution.py:197
  124.2 34.5 %copy-start.4 = (bf16[1024,256]{0,1:T(8,128)(2,1)S(1)}, bf16[1024,256]{0,1:T(8,128)(2,1)}, u32[]{:S(2)}) copy-start(bf16[1024,256]{0,1:T(8,128)(2,1)} %copy-done.3) | copy-start | bytes 1572868
  124.3 7.6 %collective-permute-start.2 = (f32[32,1024]{1,0:T(8,128)S(1)}, f32[32,1024]{1,0:T(8,128)S(1)}, u32[]{:S(2)}, u32[]{:S(2)}) collective-permute-start(f32[32,1024]{1,0:T(8,128)S(1)} %bitcast.102), channel_id=1, source_target_pairs={{0,32},{32,0},{64,96},{96,64},{128,160},{160,128},{192,224},{224,1... | collective-permute-start | bytes 393224 | tf_op jit(solution)/shard_map/ppermute | solution.py:191
  131.9 10.3 %collective-permute-start.3 = (f32[32,1024]{1,0:T(8,128)S(1)}, f32[32,1024]{1,0:T(8,128)S(1)}, u32[]{:S(2)}, u32[]{:S(2)}) collective-permute-start(f32[32,1024]{1,0:T(8,128)S(1)} %bitcast_add_fusion), channel_id=1, source_target_pairs={{0,64},{32,96},{64,0},{96,32},{128,192},{160,224},{192,128},{224,1... | collective-permute-start | bytes 393224 | tf_op jit(solution)/shard_map/ppermute | solution.py:191
  142.3 13.2 %collective-permute-start.4 = (f32[32,1024]{1,0:T(8,128)S(1)}, f32[32,1024]{1,0:T(8,128)S(1)}, u32[]{:S(2)}, u32[]{:S(2)}) collective-permute-start(f32[32,1024]{1,0:T(8,128)S(1)} %add.21), channel_id=1, source_target_pairs={{0,128},{32,160},{64,192},{96,224},{128,0},{160,32},{192,64},{224,... | collective-permute-start | bytes 393224 | tf_op jit(solution)/shard_map/ppermute | solution.py:191
  155.5 11.6 %collective-permute-start.5 = (f32[64,1024]{1,0:T(8,128)S(1)}, f32[64,1024]{1,0:T(8,128)S(1)}, u32[]{:S(2)}, u32[]{:S(2)}) collective-permute-start(f32[64,1024]{1,0:T(8,128)S(1)} %pad_maximum_fusion.1), channel_id=1, source_target_pairs={{0,256},{256,0},{1,257},{257,1},{2,258},{258,2},{3,259},{259,3},{4... | collective-permute-start | bytes 786440 | tf_op jit(solution)/shard_map/ppermute | solution.py:205
Sparse Core Ops, SparseCore 0:
  42.4 46.2 all-gather.1

commit v2 on v1

v2 whole, which is shorter than its diff:
```python
import functools

import jax
import jax.numpy as jnp
from jax import lax
from jax.experimental import pallas as pl
from jax.experimental.pallas import tpu as pltpu
from jax.sharding import Mesh
from jax.sharding import PartitionSpec as P

TENANT_COUNT = 8
GROUP = 64
ADAPTER_SCALE = 2.0
BF = jnp.bfloat16
F32 = jnp.float32


def dot(a, b, dims):
    return lax.dot_general(a, b, (dims, ((), ())), preferred_element_type=F32)


def weight_kernel(group, half_ref, level_ref, scale_ref, first_ref, kept_ref, sent_ref):
    planes, rows, width = level_ref.shape
    mid = width // 2
    near = pl.multiple_of(half_ref[0] * mid, 128)
    far = pl.multiple_of((1 - half_ref[0]) * mid, 128)

    def rounded(j, start):
        parts = []
        for g in range(rows // group):
            level = level_ref[j, g * group : (g + 1) * group, pl.ds(start, mid)].astype(F32)
            scale = scale_ref[j, g : g + 1, pl.ds(start, mid)].astype(F32)
            parts.append((level * scale).astype(BF))
        return jnp.concatenate(parts, axis=0)

    for j in range(planes):
        sent_ref[j, :, :mid] = rounded(j, far)
        sent_ref[j, :, mid:] = first_ref[j]
        kept_ref[j] = rounded(j, near).T


def weight_call(half, levels, scales, first):
    planes, rows, width = levels.shape
    mid, cols = width // 2, first.shape[2]
    vmem = pl.BlockSpec(memory_space=pltpu.VMEM)
    return pl.pallas_call(
        functools.partial(weight_kernel, GROUP),
        in_specs=[pl.BlockSpec(memory_space=pltpu.SMEM), vmem, vmem, vmem],
        out_specs=[vmem, vmem],
        out_shape=[
            jax.ShapeDtypeStruct((planes, mid, rows), BF),
            jax.ShapeDtypeStruct((planes, rows, mid + cols), BF),
        ],
        compiler_params=pltpu.CompilerParams(vmem_limit_bytes=16 * 1024 * 1024),
        cost_estimate=pl.CostEstimate(
            flops=planes * rows * width, bytes_accessed=4 * planes * rows * width, transcendentals=0
        ),
    )(half, levels, scales, first)


def pair_kernel(
    rank, tile, own, half_ref, z_ref, rows_ref, cols_ref, kept_ref, got_ref, first_ref,
    dx_ref, back_ref, turned_ref
):
    ring, planes, hid, wide = z_ref.shape
    room, depth, width = dx_ref.shape[2] * 128 // kept_ref.shape[2], kept_ref.shape[1], kept_ref.shape[2]
    slots = dx_ref.shape[1] * room
    tiles, cols = slots // tile, wide - slots
    some, full = tile // room, width // 128
    for j in range(planes):
        turned_ref[j] = got_ref[j, :, :depth].T
    at = own
    half = half_ref[0]
    lane = lax.broadcasted_iota(jnp.int32, (tile, cols), 1)

    def step(i, carry):
        place = pl.ds(pl.multiple_of(i * tile, tile), tile)
        gate = rows_ref[place, at : at + 1].astype(F32)
        tenant = rows_ref[place, at + 1 : at + 2].astype(F32)
        tenant_row = cols_ref[own + 1 : own + 2, place].astype(F32)
        mine = (lane // rank).astype(F32) == tenant
        z, scaled = [], []
        for j in range(planes):
            z.append(z_ref[:, j, :, place].reshape(ring * hid, tile))
            second = z_ref[:, j, :, slots:].reshape(ring * hid, cols)
            back = dot(z[j], second, ((0,), (0,)))
            scaled.append(jnp.where(mine, back * (ADAPTER_SCALE * gate), 0.0).astype(BF))
            across = dot(second, z[j], ((0,), (0,)))
            total = jnp.zeros((rank, tile), F32)
            for t in range(cols // rank):
                part = across[t * rank : (t + 1) * rank]
                total += jnp.where(tenant_row == float(t), part, 0.0)
            back_ref[j * rank : (j + 1) * rank, place] = total
        firsts = [first_ref[j] for j in range(planes)], [got_ref[j, :, depth:] for j in range(planes)]
        both = ((half, kept_ref, firsts[0]), (1 - half, turned_ref, firsts[1]))
        from_experts = pl.ds(i * some, some)
        for where, weight, first in both:
            frozen = sum(dot(z[j], weight[j], ((0,), (0,))) for j in range(planes))
            extra = sum(dot(scaled[j], first[j], ((1,), (1,))) for j in range(planes))
            dx = (gate * frozen + extra).astype(BF).reshape(some, room, width)
            for c in range(full):
                dx_ref[where, from_experts, c * room : (c + 1) * room, :] = dx[:, :, c * 128 : (c + 1) * 128]
            rest = dx[:, :, full * 128 :]
            rest = jnp.concatenate([rest[:, : room // 2], rest[:, room // 2 :]], axis=2)
            dx_ref[where, from_experts, full * room :, :] = rest
        return carry

    lax.fori_loop(0, tiles, step, 0)


def pair_call(half, gathered, got_z, across_z, kept, got, first, rank, own, slots, experts):
    ring, planes, hid, wide = gathered.shape
    cols = wide - slots
    depth, width = kept.shape[1:]
    tile = 256 if slots % 256 == 0 else slots
    vmem = pl.BlockSpec(memory_space=pltpu.VMEM)
    return pl.pallas_call(
        functools.partial(pair_kernel, rank, tile, own),
        in_specs=[
            pl.BlockSpec(memory_space=pltpu.SMEM),
            vmem,
            vmem,
            vmem,
            vmem,
            vmem,
            vmem,
        ],
        out_specs=[vmem, vmem],
        out_shape=[
            jax.ShapeDtypeStruct((2, experts, slots // experts * width // 128, 128), BF),
            jax.ShapeDtypeStruct((planes * rank, slots), F32),
        ],
        scratch_shapes=[pltpu.VMEM((planes, depth, width), BF)],
        compiler_params=pltpu.CompilerParams(vmem_limit_bytes=24 * 1024 * 1024),
        cost_estimate=pl.CostEstimate(
            flops=2 * slots * planes * depth * (2 * width + 2 * cols),
            bytes_accessed=2 * planes * depth * (wide + 2 * width) + 4 * slots * width,
            transcendentals=0,
        ),
    )(half, gathered, got_z, across_z, kept, got, first)


def combine_kernel(got_ref, select_ref, out_ref):
    halves, experts, _, lanes = got_ref.shape
    room, toks = select_ref.shape[1:]
    full = out_ref.shape[0] // lanes

    def total(start, size, chosen):
        parts = [got_ref[h, :, start : start + size, :] for h in range(halves)]
        parts = [p.reshape(experts * size, lanes) for p in parts]
        return sum(dot(p, chosen, ((0,), (0,))) for p in parts)

    select = select_ref[...].reshape(experts * room, toks)
    for c in range(full):
        out_ref[c * lanes : (c + 1) * lanes, :] = total(c * room, room, select).astype(BF)
    low = select_ref[:, : room // 2].reshape(experts * room // 2, toks)
    high = select_ref[:, room // 2 :].reshape(experts * room // 2, toks)
    first = total(full * room, room // 2, low)[: lanes // 2]
    second = total(full * room, room // 2, high)[lanes // 2 :]
    out_ref[full * lanes :, :] = (first + second).astype(BF)


def combine_call(got, select, width):
    vmem = pl.BlockSpec(memory_space=pltpu.VMEM)
    return pl.pallas_call(
        combine_kernel,
        in_specs=[vmem, vmem],
        out_specs=vmem,
        out_shape=jax.ShapeDtypeStruct((width, select.shape[2]), BF),
        compiler_params=pltpu.CompilerParams(vmem_limit_bytes=16 * 1024 * 1024),
        cost_estimate=pl.CostEstimate(
            flops=2 * got.size * select.shape[2], bytes_accessed=4 * got.size, transcendentals=0
        ),
    )(got, select)


def on_device(
    projection_gradient,
    acts,
    routes,
    gates,
    tenants,
    levels,
    scales,
    adapter_first_factors,
    adapter_second_factors,
):
    experts = lax.axis_size("expert")
    ring = lax.axis_size("y")
    half = lax.axis_index("xh")
    planes, hid, topk, toks = projection_gradient.shape
    width_rows = acts.shape[0]
    rank = adapter_first_factors.shape[3] // TENANT_COUNT
    cols = TENANT_COUNT * rank
    capacity = 5 * toks * topk // (4 * experts)
    room = -(-capacity // 16) * 16
    slots = experts * room
    own = planes * hid

    expert_ids = lax.broadcasted_iota(jnp.int32, (experts, toks), 0)
    named = [routes[:, k][None, :] == expert_ids for k in range(topk)]
    member = functools.reduce(jnp.logical_or, named).astype(BF)
    before = (
        lax.broadcasted_iota(jnp.int32, (toks, toks), 0)
        < lax.broadcasted_iota(jnp.int32, (toks, toks), 1)
    ).astype(BF)
    place = dot(member, before, ((1,), (0,))).astype(jnp.int32) + expert_ids * room
    position = [jnp.sum(jnp.where(m, place, 0), axis=0) for m in named]
    slot_ids = lax.broadcasted_iota(jnp.int32, (slots, toks), 0)
    chosen = [slot_ids == p[None, :] for p in position]
    select = jnp.concatenate([c.astype(BF) for c in chosen], axis=1)
    select_tok = functools.reduce(jnp.logical_or, chosen).astype(BF)

    side = 64
    sent = jnp.concatenate(
        [
            projection_gradient.reshape(own, topk * toks),
            gates.T.reshape(1, topk * toks),
            jnp.tile(tenants.astype(BF)[None, :], (1, topk)),
            jnp.zeros((side - 2, topk * toks), BF),
        ],
        axis=0,
    )
    send_z = dot(select, sent, ((1,), (1,))).astype(BF).reshape(experts, room, -1)
    send_z, levels, scales, acts = lax.optimization_barrier((send_z, levels, scales, acts))
    got_z = lax.all_to_all(send_z, "expert", 0, 0, tiled=True).reshape(slots, -1)

    adapter_first = adapter_first_factors[0]
    adapter_second = adapter_second_factors[0].reshape(own, cols)
    swap = [(0, 1), (1, 0)]
    kept_w, send_w = weight_call(half.reshape(1), levels[0], scales[0], adapter_first)
    send_x = dot(select_tok, acts, ((1,), (1,))).astype(BF).reshape(experts, room, width_rows)
    got_w = lax.ppermute(send_w, "xh", swap)
    got_z, send_x, kept_w = lax.optimization_barrier((got_z, send_x, kept_w))

    across_z = got_z.T
    own_z = across_z[:own]
    payload = jnp.concatenate([own_z, adapter_second], axis=1)
    gathered = lax.all_gather(payload.reshape(planes, hid, slots + cols), "y", axis=0, tiled=False)

    got_x = lax.all_to_all(send_x, "expert", 0, 0, tiled=True).reshape(slots, width_rows)
    gate_row = across_z[own].astype(F32)
    tenant_row = across_z[own + 1].astype(F32)
    one = tenant_row[None, :] == jnp.arange(TENANT_COUNT, dtype=F32)[:, None]
    down = lax.dot_general(
        adapter_first, got_x, (((1,), (1,)), ((), ())), preferred_element_type=F32
    ).reshape(planes, TENANT_COUNT, rank, slots)
    down = jnp.sum(jnp.where(one[None, :, None, :], down, 0.0), axis=1).reshape(
        planes * rank, slots
    )
    exchanges = [[(i, i ^ (1 << k)) for i in range(ring)] for k in range(ring.bit_length() - 1)]
    down = down + lax.ppermute(down, "y", exchanges[0])
    down, got_w = lax.optimization_barrier((down, got_w))
    down = down + lax.ppermute(down, "y", exchanges[1])
    down, got_w = lax.optimization_barrier((down, got_w))

    pair_dx, back = pair_call(
        half.reshape(1), gathered, got_z, across_z, kept_w, got_w, adapter_first,
        rank, own, slots, experts
    )
    returned = lax.all_to_all(
        pair_dx.reshape((2 * experts,) + pair_dx.shape[2:]), ("xh", "expert"), 0, 0, tiled=True
    ).reshape(pair_dx.shape)
    for pairs in exchanges[2:]:
        down = down + lax.ppermute(down, "y", pairs)
    ranks = jnp.concatenate([down, back], axis=0)
    ranks = ranks + lax.ppermute(ranks, "xh", swap)
    scaled = (ranks * (ADAPTER_SCALE * gate_row)[None, :]).astype(BF)
    spread = jnp.where(
        one[None, :, None, :], scaled.reshape(2 * planes, 1, rank, slots), jnp.zeros((), BF)
    ).reshape(2, planes, cols, slots)
    second_grad = jnp.stack(
        [
            dot(own_z[j * hid : (j + 1) * hid], spread[0, j], ((1,), (1,)))
            for j in range(planes)
        ]
    )
    first_grad = jnp.stack([dot(got_x, spread[1, j].T, ((0,), (0,))) for j in range(planes)])
    returned, first_grad, second_grad = lax.optimization_barrier((returned, first_grad, second_grad))
    input_grad = combine_call(returned, select_tok.reshape(experts, room, toks), width_rows)
    return input_grad, first_grad[None], second_grad[None]


def solution(mesh):
    groups, experts = mesh.devices.shape
    split = Mesh(mesh.devices.reshape(2, groups // 2, experts), ("xh", "y", "expert"))
    dp = ("xh", "y")
    factors = P("expert", None, dp, None)
    return jax.shard_map(
        on_device,
        mesh=split,
        in_specs=(
            P(None, dp, None, "expert"),
            P(dp, "expert"),
            P("expert", None),
            P("expert", None),
            P("expert"),
            factors,
            factors,
            factors,
            factors,
        ),
        out_specs=(P(dp, "expert"), factors, factors),
        check_vma=False,
    )
```

time: 182 us -> 164 us (0.901)
  the two profiles are of different devices: /device:TPU:62 before, /device:TPU:1 now
where the time goes in v2:
time: 164 us; the launch traced here: 163 us
  waiting for transfers between devices  68.2 us (42%)
  starting transfers between devices  50.8 us (31%)
  between operations  14.4 us (9%)
  Pallas kernels  12.5 us (8%)
  local copies, waits for them, and re-layouts  8.58 us (5%)
  matrix products  4.87 us (3%)
  other arithmetic  4.11 us (3%)
    all_to_all x1, waiting for transfers between devices, on_device(): lax.all_to_all(send_x, 'expert', 0, 0, tiled=True)  17 us
    all_to_all x1, starting transfers between devices, on_device(): lax.all_to_all(send_z, 'expert', 0, 0, tiled=True).reshape(slots, -1)  12.9 us
    all_to_all x1, starting transfers between devices, on_device(): lax.all_to_all(pair_dx.reshape((2 * experts,) + pair_dx.shape[2:]), ('xh'...  10.2 us
    all_to_all x1, waiting for transfers between devices, on_device(): lax.all_to_all(send_z, 'expert', 0, 0, tiled=True).reshape(slots, -1)  10 us
    ppermute x1, waiting for transfers between devices, on_device(): ranks = ranks + lax.ppermute(ranks, 'xh', swap)  9.97 us
    pallas_call x1, Pallas kernels, pair_call(): pl.pallas_call(functools.partial(pair_kernel, rank, tile, own), in_specs=...  9.08 us
    ppermute x1, waiting for transfers between devices, on_device(): down = down + lax.ppermute(down, 'y', exchanges[1])  8.33 us
    ppermute x1, waiting for transfers between devices, on_device(): down = down + lax.ppermute(down, 'y', exchanges[0])  6.14 us
  transfers between devices with their start and end apart: 9, of which 8 were waited for; matrix products, arithmetic and copies ran while one was open for 5% of the time, Pallas kernels for 1%

profile of v2, /device:TPU:1, one launch (start us, length us, event | category | flops | bytes accessed | tf_op | source)
XLA Modules:
  0.0 163.4 jit_solution(8203605595682991280)
XLA Ops:
  7.2 0.8 slice_reduce_fusion.1
  8.0 1.0 copy.25
  9.0 0.7 convert_element_type.30
  9.7 0.7 copy.26
  10.4 0.2 select_reduce_fusion.2
  10.6 0.5 iota_compare_fusion
  11.1 0.1 pad.11.clone
  11.2 1.5 fusion.9
  12.7 12.9 %all-to-all-start = ((bf16[32,32,256]{2,1,0:T(8,128)(2,1)}), bf16[32,32,256]{2,1,0:T(8,128)(2,1)S(1)}, u32[]{:S(2)}, u32[]{:S(2)}) async-start(bf16[32,32,256]{2,1,0:T(8,128)(2,1)} %bitcast.4), calls=%async_computation | async-start | bytes 1048576 | tf_op jit(solution)/shard_map/all_to_all | solution.py:226
  25.6 0.0 all-gather.2.cloned.1.call-start
  25.7 1.5 fusion.6
  27.2 2.3 %copy.19 = bf16[1024,320]{1,0:T(8,128)(2,1)} copy(bf16[1024,320]{0,1:T(8,128)(2,1)} %fusion.6) | data formatting | bytes 1310720 | tf_op jit(solution)/shard_map/convert_element_type | solution.py:232
  29.4 1.6 %shard_map.112 = (bf16[2,768,320]{2,1,0:T(8,128)(2,1)S(1)}, bf16[2,320,896]{2,1,0:T(8,128)(2,1)}) custom-call(s32[1]{0:T(128)} %bitcast.2.half_ref, bf16[2,320,1536]{2,1,0:T(8,128)(2,1)S(1)} %bitcast.69, bf16[2,5,1536]{2,1,0:T(8,128)(2,1)S(1)} %bitcast.78, bf16[2,320,128]{2,1,0:T(8,128)(2,1)S(1)} %bitcast.76), custom_call_target="tpu_custom_call" | custom-call | flops 983040 | bytes 3932160 | tf_op jit(solution)/shard_map/pallas_call | solution.py:46
  31.1 1.0 copy-done.4
  32.1 10.0 %all-to-all-done = bf16[32,32,256]{2,1,0:T(8,128)(2,1)S(1)} async-done(((bf16[32,32,256]{2,1,0:T(8,128)(2,1)}), bf16[32,32,256]{2,1,0:T(8,128)(2,1)S(1)}, u32[]{:S(2)}, u32[]{:S(2)}) %all-to-all-start) | async-done | bytes 524320 | tf_op jit(solution)/shard_map/all_to_all | solution.py:226
  42.2 0.2 copy.21
  42.4 0.9 pad_maximum_fusion
  43.3 0.0 all-gather.2.cloned.1.call-update
  43.3 5.7 %all-to-all-start.1 = ((bf16[32,32,320]{2,1,0:T(8,128)(2,1)}), bf16[32,32,320]{2,1,0:T(8,128)(2,1)S(1)}, u32[]{:S(2)}, u32[]{:S(2)}) async-start(bf16[32,32,320]{2,1,0:T(8,128)(2,1)} %bitcast.6), calls=%async_computation.1 | async-start | bytes 1572864 | tf_op jit(solution)/shard_map/all_to_all | solution.py:241
  49.0 4.4 %collective-permute-start.1 = (bf16[2,320,896]{2,1,0:T(8,128)(2,1)}, bf16[2,320,896]{2,1,0:T(8,128)(2,1)}, u32[]{:S(2)}, u32[]{:S(2)}) collective-permute-start(bf16[2,320,896]{2,1,0:T(8,128)(2,1)} %get-tuple-element.29), channel_id=1, source_target_pairs={{0,256},{256,0},{1,257},{257,1},{2,258},{258,2},{3,259},{259,3},{4... | collective-permute-start | bytes 3440648 | tf_op jit(solution)/shard_map/ppermute | solution.py:233
  53.4 17.0 %all-to-all-done.1 = bf16[32,32,320]{2,1,0:T(8,128)(2,1)S(1)} async-done(((bf16[32,32,320]{2,1,0:T(8,128)(2,1)}), bf16[32,32,320]{2,1,0:T(8,128)(2,1)S(1)}, u32[]{:S(2)}, u32[]{:S(2)}) %all-to-all-start.1) | async-done | bytes 655392 | tf_op jit(solution)/shard_map/all_to_all | solution.py:241
  70.4 0.5 fusion.29
  70.9 0.1 select_reduce_fusion
  71.0 0.3 copy-done.6
  71.3 3.2 %collective-permute-start = (f32[32,1024]{1,0:T(8,128)S(1)}, f32[32,1024]{1,0:T(8,128)S(1)}, u32[]{:S(2)}, u32[]{:S(2)}) collective-permute-start(f32[32,1024]{1,0:T(8,128)S(1)} %bitcast.85), channel_id=1, source_target_pairs={{0,32},{32,0},{64,96},{96,64},{128,160},{160,128},{192,224},{224,1... | collective-permute-start | bytes 393224 | tf_op jit(solution)/shard_map/ppermute | solution.py:252
  74.5 6.1 %collective-permute-done = f32[32,1024]{1,0:T(8,128)S(1)} collective-permute-done((f32[32,1024]{1,0:T(8,128)S(1)}, f32[32,1024]{1,0:T(8,128)S(1)}, u32[]{:S(2)}, u32[]{:S(2)}) %collective-permute-start) | collective-permute-done | bytes 131104 | tf_op jit(solution)/shard_map/ppermute | solution.py:252
  80.6 6.1 %collective-permute-done.1.got_ref = bf16[2,320,896]{2,1,0:T(8,128)(2,1)} collective-permute-done((bf16[2,320,896]{2,1,0:T(8,128)(2,1)}, bf16[2,320,896]{2,1,0:T(8,128)(2,1)}, u32[]{:S(2)}, u32[]{:S(2)}) %collective-permute-start.1) | collective-permute-done | bytes 1146912 | tf_op jit(solution)/shard_map/ppermute | solution.py:233
  86.7 4.2 %collective-permute-start.2 = (f32[32,1024]{1,0:T(8,128)S(1)}, f32[32,1024]{1,0:T(8,128)S(1)}, u32[]{:S(2)}, u32[]{:S(2)}) collective-permute-start(f32[32,1024]{1,0:T(8,128)S(1)} %bitcast_add_fusion), channel_id=1, source_target_pairs={{0,64},{32,96},{64,0},{96,32},{128,192},{160,224},{192,128},{224,1... | collective-permute-start | bytes 393224 | tf_op jit(solution)/shard_map/ppermute | solution.py:254
  90.9 8.3 %collective-permute-done.2 = f32[32,1024]{1,0:T(8,128)S(1)} collective-permute-done((f32[32,1024]{1,0:T(8,128)S(1)}, f32[32,1024]{1,0:T(8,128)S(1)}, u32[]{:S(2)}, u32[]{:S(2)}) %collective-permute-start.2) | collective-permute-done | bytes 131104 | tf_op jit(solution)/shard_map/ppermute | solution.py:254
  99.3 0.0 all-gather.2.cloned.1.call-done.z_ref
  99.3 2.0 %copy-done.3 = bf16[8,2,96,1152]{3,2,1,0:T(8,128)(2,1)S(1)} copy-done((bf16[8,2,96,1152]{3,2,1,0:T(8,128)(2,1)S(1)}, bf16[8,2,96,1152]{3,2,1,0:T(8,128)(2,1)}, u32[]{:S(2)}) %copy-start.3) | copy-done | bytes 3538968
  101.3 9.1 %shard_map.113 = (bf16[2,32,80,128]{3,2,1,0:T(8,128)(2,1)}, f32[32,1024]{1,0:T(8,128)S(1)}) custom-call(s32[1]{0:T(128)} %bitcast.2.half_ref, bf16[8,2,96,1152]{3,2,1,0:T(8,128)(2,1)S(1)} %copy-done.3, bf16[1024,256]{1,0:T(8,128)(2,1)S(1)} %bitcast.68, bf16[256,1024]{1,0:T(8,128)(2,1)S(1)} %bitcast.72, bf16[2,768,320]{2,1,0:T(8,128)(2,1)S(1)} %copy-done.5, ...), custom_call_target="tpu_custom_call" | custom-call | flops 2818572288 | bytes 6815744 | tf_op jit(solution)/shard_map/pallas_call | solution.py:117
  110.4 10.2 %all-to-all-start.2 = ((bf16[64,80,128]{2,1,0:T(8,128)(2,1)}), bf16[64,80,128]{2,1,0:T(8,128)(2,1)S(1)}, u32[]{:S(2)}, u32[]{:S(2)}) async-start(bf16[64,80,128]{2,1,0:T(8,128)(2,1)} %bitcast.17), calls=%async_computation.2 | async-start | bytes 2621440 | tf_op jit(solution)/shard_map/all_to_all | solution.py:261
  120.6 5.3 %collective-permute-start.3 = (f32[32,1024]{1,0:T(8,128)S(1)}, f32[32,1024]{1,0:T(8,128)S(1)}, u32[]{:S(2)}, u32[]{:S(2)}) collective-permute-start(f32[32,1024]{1,0:T(8,128)S(1)} %add.22), channel_id=1, source_target_pairs={{0,128},{32,160},{64,192},{96,224},{128,0},{160,32},{192,64},{224,... | collective-permute-start | bytes 393224 | tf_op jit(solution)/shard_map/ppermute | solution.py:265
  125.9 5.1 %collective-permute-done.3 = f32[32,1024]{1,0:T(8,128)S(1)} collective-permute-done((f32[32,1024]{1,0:T(8,128)S(1)}, f32[32,1024]{1,0:T(8,128)S(1)}, u32[]{:S(2)}, u32[]{:S(2)}) %collective-permute-start.3) | collective-permute-done | bytes 131104 | tf_op jit(solution)/shard_map/ppermute | solution.py:265
  131.1 5.0 %collective-permute-start.4 = (f32[64,1024]{1,0:T(8,128)S(1)}, f32[64,1024]{1,0:T(8,128)S(1)}, u32[]{:S(2)}, u32[]{:S(2)}) collective-permute-start(f32[64,1024]{1,0:T(8,128)S(1)} %pad_maximum_fusion.2), channel_id=1, source_target_pairs={{0,256},{256,0},{1,257},{257,1},{2,258},{258,2},{3,259},{259,3},{4... | collective-permute-start | bytes 786440 | tf_op jit(solution)/shard_map/ppermute | solution.py:267
  136.1 0.3 or_convert_fusion.select_ref
  136.4 10.0 %collective-permute-done.4 = f32[64,1024]{1,0:T(8,128)S(1)} collective-permute-done((f32[64,1024]{1,0:T(8,128)S(1)}, f32[64,1024]{1,0:T(8,128)S(1)}, u32[]{:S(2)}, u32[]{:S(2)}) %collective-permute-start.4) | collective-permute-done | bytes 262176 | tf_op jit(solution)/shard_map/ppermute | solution.py:267
  146.4 0.1 broadcast_in_dim.69
  146.6 0.1 broadcast_select_fusion
  146.7 0.2 convolution_bitcast_fusion.3
  146.9 0.2 convolution_bitcast_fusion.2
  147.2 0.7 pad_maximum_fusion.3
  147.8 0.4 convolution_bitcast_fusion.1
  148.2 0.4 convolution_bitcast_fusion
  148.6 0.7 pad_maximum_fusion.1
  149.4 5.4 %all-to-all-done.2 = bf16[64,80,128]{2,1,0:T(8,128)(2,1)S(1)} async-done(((bf16[64,80,128]{2,1,0:T(8,128)(2,1)}), bf16[64,80,128]{2,1,0:T(8,128)(2,1)S(1)}, u32[]{:S(2)}, u32[]{:S(2)}) %all-to-all-start.2) | async-done | bytes 1310752 | tf_op jit(solution)/shard_map/all_to_all | solution.py:261
  154.8 1.7 %shard_map.114 = bf16[320,384]{1,0:T(8,128)(2,1)} custom-call(bf16[2,32,80,128]{3,2,1,0:T(8,128)(2,1)S(1)} %bitcast.66, bf16[32,32,384]{2,1,0:T(8,128)(2,1)S(1)} %or_convert_fusion.select_ref), custom_call_target="tpu_custom_call" | custom-call | flops 503316480 | bytes 2621440 | tf_op jit(solution)/shard_map/pallas_call | solution.py:165
  (33 shorter events, 0.3 us)
Async XLA Ops:
  7.2 18.5 %copy-start = (bf16[320,384]{1,0:T(8,128)(2,1)S(1)}, bf16[320,384]{1,0:T(8,128)(2,1)}, u32[]{:S(2)}) copy-start(bf16[320,384]{1,0:T(8,128)(2,1)} %param.10) | copy-start | bytes 737284
  11.2 14.5 %copy-start.9 = (bf16[1,2,5,1536]{3,1,2,0:T(2,128)(2,1)S(1)}, bf16[1,2,5,1536]{3,1,2,0:T(2,128)(2,1)}, u32[]{:S(2)}) copy-start(bf16[1,2,5,1536]{3,1,2,0:T(2,128)(2,1)} %param.15) | copy-start | bytes 92164
  12.7 29.5 %all-to-all-start = ((bf16[32,32,256]{2,1,0:T(8,128)(2,1)}), bf16[32,32,256]{2,1,0:T(8,128)(2,1)S(1)}, u32[]{:S(2)}, u32[]{:S(2)}) async-start(bf16[32,32,256]{2,1,0:T(8,128)(2,1)} %bitcast.4), calls=%async_computation | async-start | bytes 1048576 | tf_op jit(solution)/shard_map/all_to_all | solution.py:226
  25.6 73.7 %all-gather.2.cloned.1.call-start = ((), (), s32[]{:S(2)}) async-start(), calls=%async_computation.3 | async-start | bytes 3981312 | tf_op jit(solution)/shard_map/all_gather | solution.py:239
  25.7 3.8 %copy-start.1 = (bf16[1,2,320,1536]{3,2,1,0:T(8,128)(2,1)S(1)}, bf16[1,2,320,1536]{3,2,1,0:T(8,128)(2,1)}, u32[]{:S(2)}) copy-start(bf16[1,2,320,1536]{3,2,1,0:T(8,128)(2,1)} %param.14) | copy-start | bytes 5898244
  25.7 3.8 %copy-start.2 = (bf16[1,2,320,128]{3,2,1,0:T(8,128)(2,1)S(1)}, bf16[1,2,320,128]{3,2,1,0:T(8,128)(2,1)}, u32[]{:S(2)}) copy-start(bf16[1,2,320,128]{3,2,1,0:T(8,128)(2,1)} %param.16) | copy-start | bytes 491524
  29.4 13.0 %copy-start.8 = (bf16[1,2,96,128]{3,2,1,0:T(8,128)(2,1)S(1)}, bf16[1,2,96,128]{3,2,1,0:T(8,128)(2,1)}, u32[]{:S(2)}) copy-start(bf16[1,2,96,128]{3,2,1,0:T(8,128)(2,1)} %param.17) | copy-start | bytes 147460
  31.1 1.0 copy-start.4
  43.3 27.1 %all-to-all-start.1 = ((bf16[32,32,320]{2,1,0:T(8,128)(2,1)}), bf16[32,32,320]{2,1,0:T(8,128)(2,1)S(1)}, u32[]{:S(2)}, u32[]{:S(2)}) async-start(bf16[32,32,320]{2,1,0:T(8,128)(2,1)} %bitcast.6), calls=%async_computation.1 | async-start | bytes 1572864 | tf_op jit(solution)/shard_map/all_to_all | solution.py:241
  49.0 37.7 %collective-permute-start.1 = (bf16[2,320,896]{2,1,0:T(8,128)(2,1)}, bf16[2,320,896]{2,1,0:T(8,128)(2,1)}, u32[]{:S(2)}, u32[]{:S(2)}) collective-permute-start(bf16[2,320,896]{2,1,0:T(8,128)(2,1)} %get-tuple-element.29), channel_id=1, source_target_pairs={{0,256},{256,0},{1,257},{257,1},{2,258},{258,2},{3,259},{259,3},{4... | collective-permute-start | bytes 3440648 | tf_op jit(solution)/shard_map/ppermute | solution.py:233
  70.4 0.9 copy-start.6
  70.4 28.9 %copy-start.5 = (bf16[2,768,320]{2,1,0:T(8,128)(2,1)S(1)}, bf16[2,768,320]{2,1,0:T(8,128)(2,1)}, u32[]{:S(2)}) copy-start(bf16[2,768,320]{2,1,0:T(8,128)(2,1)} %copy-done.4) | copy-start | bytes 2949124
  71.3 9.3 %collective-permute-start = (f32[32,1024]{1,0:T(8,128)S(1)}, f32[32,1024]{1,0:T(8,128)S(1)}, u32[]{:S(2)}, u32[]{:S(2)}) collective-permute-start(f32[32,1024]{1,0:T(8,128)S(1)} %bitcast.85), channel_id=1, source_target_pairs={{0,32},{32,0},{64,96},{96,64},{128,160},{160,128},{192,224},{224,1... | collective-permute-start | bytes 393224 | tf_op jit(solution)/shard_map/ppermute | solution.py:252
  86.7 12.5 %collective-permute-start.2 = (f32[32,1024]{1,0:T(8,128)S(1)}, f32[32,1024]{1,0:T(8,128)S(1)}, u32[]{:S(2)}, u32[]{:S(2)}) collective-permute-start(f32[32,1024]{1,0:T(8,128)S(1)} %bitcast_add_fusion), channel_id=1, source_target_pairs={{0,64},{32,96},{64,0},{96,32},{128,192},{160,224},{192,128},{224,1... | collective-permute-start | bytes 393224 | tf_op jit(solution)/shard_map/ppermute | solution.py:254
  99.3 2.0 %copy-start.3 = (bf16[8,2,96,1152]{3,2,1,0:T(8,128)(2,1)S(1)}, bf16[8,2,96,1152]{3,2,1,0:T(8,128)(2,1)}, u32[]{:S(2)}) copy-start(bf16[8,2,96,1152]{3,2,1,0:T(8,128)(2,1)} %all-gather.2.cloned.1.call-done.z_ref) | copy-start | bytes 10616836
  110.4 44.4 %all-to-all-start.2 = ((bf16[64,80,128]{2,1,0:T(8,128)(2,1)}), bf16[64,80,128]{2,1,0:T(8,128)(2,1)S(1)}, u32[]{:S(2)}, u32[]{:S(2)}) async-start(bf16[64,80,128]{2,1,0:T(8,128)(2,1)} %bitcast.17), calls=%async_computation.2 | async-start | bytes 2621440 | tf_op jit(solution)/shard_map/all_to_all | solution.py:261
  120.6 10.4 %collective-permute-start.3 = (f32[32,1024]{1,0:T(8,128)S(1)}, f32[32,1024]{1,0:T(8,128)S(1)}, u32[]{:S(2)}, u32[]{:S(2)}) collective-permute-start(f32[32,1024]{1,0:T(8,128)S(1)} %add.22), channel_id=1, source_target_pairs={{0,128},{32,160},{64,192},{96,224},{128,0},{160,32},{192,64},{224,... | collective-permute-start | bytes 393224 | tf_op jit(solution)/shard_map/ppermute | solution.py:265
  131.1 15.3 %collective-permute-start.4 = (f32[64,1024]{1,0:T(8,128)S(1)}, f32[64,1024]{1,0:T(8,128)S(1)}, u32[]{:S(2)}, u32[]{:S(2)}) collective-permute-start(f32[64,1024]{1,0:T(8,128)S(1)} %pad_maximum_fusion.2), channel_id=1, source_target_pairs={{0,256},{256,0},{1,257},{257,1},{2,258},{258,2},{3,259},{259,3},{4... | collective-permute-start | bytes 786440 | tf_op jit(solution)/shard_map/ppermute | solution.py:267
  146.6 1.3 copy-start.7
Sparse Core Ops, SparseCore 0:
  43.4 50.6 all-gather.1

commit v3 on v2

--- a/solution.py
+++ b/solution.py
@@ -17,6 +17,51 @@
 
 def dot(a, b, dims):
     return lax.dot_general(a, b, (dims, ((), ())), preferred_element_type=F32)
+
+
+def route_kernel(room, side, route_ref, gate_ref, tenant_ref, grad_ref, send_ref, select_ref, full_ref):
+    topk, toks = route_ref.shape
+    own, slots = grad_ref.shape[0], send_ref.shape[0]
+    expert_ids = lax.broadcasted_iota(jnp.int32, (slots // room, toks), 0)
+    named = [route_ref[k : k + 1, :] == expert_ids for k in range(topk)]
+    member = sum(jnp.where(m, 1.0, 0.0) for m in named).astype(BF)
+    row = lax.broadcasted_iota(jnp.int32, (toks, toks), 0)
+    before = jnp.where(row < lax.broadcasted_iota(jnp.int32, (toks, toks), 1), 1.0, 0.0).astype(BF)
+    place = dot(member, before, ((1,), (0,))).astype(jnp.int32) + expert_ids * room
+    slot_ids = lax.broadcasted_iota(jnp.int32, (slots, toks), 0)
+    line = lax.broadcasted_iota(jnp.int32, (side, toks), 0)
+    tenant = tenant_ref[...].astype(F32)
+    total, either = 0.0, 0.0
+    for k in range(topk):
+        position = jnp.sum(jnp.where(named[k], place, 0), axis=0, keepdims=True)
+        chosen = jnp.where(slot_ids == position, 1.0, 0.0)
+        either = either + chosen
+        gate = gate_ref[k : k + 1, :].astype(F32)
+        extra = jnp.where(line == 0, gate, jnp.where(line == 1, tenant, 0.0))
+        full_ref[:own, :] = grad_ref[:, k * toks : (k + 1) * toks]
+        full_ref[own:, :] = extra.astype(BF)
+        total = total + dot(chosen.astype(BF), full_ref[...], ((1,), (1,)))
+    send_ref[...] = total.astype(BF)
+    select_ref[...] = either.astype(BF)
+
+
+def route_call(routes, gates, tenants, grads, experts, room, side):
+    toks, own, slots = tenants.shape[1], grads.shape[0], experts * room
+    vmem = pl.BlockSpec(memory_space=pltpu.VMEM)
+    return pl.pallas_call(
+        functools.partial(route_kernel, room, side),
+        in_specs=[vmem] * 4,
+        out_specs=[vmem, vmem],
+        out_shape=[
+            jax.ShapeDtypeStruct((slots, own + side), BF),
+            jax.ShapeDtypeStruct((slots, toks), BF),
+        ],
+        scratch_shapes=[pltpu.VMEM((own + side, toks), BF)],
+        compiler_params=pltpu.CompilerParams(vmem_limit_bytes=16 * 1024 * 1024),
+        cost_estimate=pl.CostEstimate(
+            flops=4 * slots * toks * (own + side), bytes_accessed=4 * slots * toks, transcendentals=0
+        ),
+    )(routes, gates, tenants, grads)
 
 
 def weight_kernel(group, half_ref, level_ref, scale_ref, first_ref, kept_ref, sent_ref):
@@ -81,11 +126,11 @@
         mine = (lane // rank).astype(F32) == tenant
         z, scaled = [], []
         for j in range(planes):
-            z.append(z_ref[:, j, :, place].reshape(ring * hid, tile))
+            z.append(z_ref[:, j, :, place].reshape(ring * hid, tile).T)
             second = z_ref[:, j, :, slots:].reshape(ring * hid, cols)
-            back = dot(z[j], second, ((0,), (0,)))
+            back = dot(z[j], second, ((1,), (0,)))
             scaled.append(jnp.where(mine, back * (ADAPTER_SCALE * gate), 0.0).astype(BF))
-            across = dot(second, z[j], ((0,), (0,)))
+            across = back.T
             total = jnp.zeros((rank, tile), F32)
             for t in range(cols // rank):
                 part = across[t * rank : (t + 1) * rank]
@@ -95,7 +140,7 @@
         both = ((half, kept_ref, firsts[0]), (1 - half, turned_ref, firsts[1]))
         from_experts = pl.ds(i * some, some)
         for where, weight, first in both:
-            frozen = sum(dot(z[j], weight[j], ((0,), (0,))) for j in range(planes))
+            frozen = sum(dot(z[j], weight[j], ((1,), (0,))) for j in range(planes))
             extra = sum(dot(scaled[j], first[j], ((1,), (1,))) for j in range(planes))
             dx = (gate * frozen + extra).astype(BF).reshape(some, room, width)
             for c in range(full):
@@ -197,31 +242,15 @@
     slots = experts * room
     own = planes * hid
 
-    expert_ids = lax.broadcasted_iota(jnp.int32, (experts, toks), 0)
-    named = [routes[:, k][None, :] == expert_ids for k in range(topk)]
-    member = functools.reduce(jnp.logical_or, named).astype(BF)
-    before = (
-        lax.broadcasted_iota(jnp.int32, (toks, toks), 0)
-        < lax.broadcasted_iota(jnp.int32, (toks, toks), 1)
-    ).astype(BF)
-    place = dot(member, before, ((1,), (0,))).astype(jnp.int32) + expert_ids * room
-    position = [jnp.sum(jnp.where(m, place, 0), axis=0) for m in named]
-    slot_ids = lax.broadcasted_iota(jnp.int32, (slots, toks), 0)
-    chosen = [slot_ids == p[None, :] for p in position]
-    select = jnp.concatenate([c.astype(BF) for c in chosen], axis=1)
-    select_tok = functools.reduce(jnp.logical_or, chosen).astype(BF)
-
     side = 64
-    sent = jnp.concatenate(
-        [
-            projection_gradient.reshape(own, topk * toks),
-            gates.T.reshape(1, topk * toks),
-            jnp.tile(tenants.astype(BF)[None, :], (1, topk)),
-            jnp.zeros((side - 2, topk * toks), BF),
-        ],
-        axis=0,
-    )
-    send_z = dot(select, sent, ((1,), (1,))).astype(BF).reshape(experts, room, -1)
+    send_z, select_tok = route_call(
+        routes.T,
+        gates.T,
+        tenants.reshape(1, toks),
+        projection_gradient.reshape(own, topk * toks),
+        experts, room, side
+    )
+    send_z = send_z.reshape(experts, room, own + side)
     send_z, levels, scales, acts = lax.optimization_barrier((send_z, levels, scales, acts))
     got_z = lax.all_to_all(send_z, "expert", 0, 0, tiled=True).reshape(slots, -1)
 
@@ -248,11 +277,9 @@
     down = jnp.sum(jnp.where(one[None, :, None, :], down, 0.0), axis=1).reshape(
         planes * rank, slots
     )
-    exchanges = [[(i, i ^ (1 << k)) for i in range(ring)] for k in range(ring.bit_length() - 1)]
-    down = down + lax.ppermute(down, "y", exchanges[0])
+    down = down + lax.ppermute(down, "xh", swap)
     down, got_w = lax.optimization_barrier((down, got_w))
-    down = down + lax.ppermute(down, "y", exchanges[1])
-    down, got_w = lax.optimization_barrier((down, got_w))
+    downs = lax.all_gather(down, "y", axis=0, tiled=False)
 
     pair_dx, back = pair_call(
         half.reshape(1), gathered, got_z, across_z, kept_w, got_w, adapter_first,
@@ -261,10 +288,9 @@
     returned = lax.all_to_all(
         pair_dx.reshape((2 * experts,) + pair_dx.shape[2:]), ("xh", "expert"), 0, 0, tiled=True
     ).reshape(pair_dx.shape)
-    for pairs in exchanges[2:]:
-        down = down + lax.ppermute(down, "y", pairs)
-    ranks = jnp.concatenate([down, back], axis=0)
-    ranks = ranks + lax.ppermute(ranks, "xh", swap)
+    ranks = jnp.concatenate(
+        [jnp.sum(downs, axis=0), back + lax.ppermute(back, "xh", swap)], axis=0
+    )
     scaled = (ranks * (ADAPTER_SCALE * gate_row)[None, :]).astype(BF)
     spread = jnp.where(
         one[None, :, None, :], scaled.reshape(2 * planes, 1, rank, slots), jnp.zeros((), BF)

time: 164 us -> 158 us (0.963)
  starting transfers between devices: 50.8 us -> 43.9 us
  local copies, waits for them, and re-layouts: 8.58 us -> 11.6 us
  waiting for transfers between devices: 68.2 us -> 65.6 us
    ppermute x4 -> x2, waiting for transfers between devices: 29.6 us -> 12.9 us  [the longest x1 12.9 us: on_device(): down = down + lax.ppermute(down, 'xh', swap)]
    all_gather x0 -> x1, waiting for transfers between devices: none -> 10.8 us  [on_device(): downs = lax.all_gather(down, 'y', axis=0, tiled=False)]
    ppermute x4 -> x2, starting transfers between devices: 17.7 us -> 9.25 us  [the longest x1 4.9 us: on_device(): lax.ppermute(back, 'xh', swap)]
    all_to_all x1, waiting for transfers between devices: 5.43 us -> 11.8 us  [on_device(): lax.all_to_all(pair_dx.reshape((2 * experts,) + pair_dx.shape[2:]), ('xh'...]
    ppermute x1, waiting for transfers between devices: 6.09 us -> 0.01 us  [on_device(): got_w = lax.ppermute(send_w, 'xh', swap)]
    unnamed x24 -> x23, local copies, waits for them, and re-layouts: 5.06 us -> 9.34 us
    pallas_call x0 -> x1, Pallas kernels: none -> 1.99 us  [route_call(): pl.pallas_call(functools.partial(route_kernel, room, side), in_specs=[vme...]
    dot_general x7 -> x5, matrix products: 4.39 us -> 4.04 us  [dot(): return lax.dot_general(a, b, (dims, ((), ())), preferred_element_type=F32)]
  transfers between devices with their start and end apart: 9 -> 8, of which waited for: 8 -> 6; matrix products, arithmetic and copies ran while one was open for 5% -> 7% of each run, Pallas kernels for 1% -> 5%
where the time goes in v3:
time: 158 us
  waiting for transfers between devices  65.6 us (42%)
  starting transfers between devices  43.9 us (28%)
  between operations  14.3 us (9%)
  Pallas kernels  11.9 us (8%)
  local copies, waits for them, and re-layouts  11.6 us (7%)
  matrix products  5.67 us (4%)
  other arithmetic  4.53 us (3%)
    all_to_all x1, waiting for transfers between devices, on_device(): lax.all_to_all(send_x, 'expert', 0, 0, tiled=True)  17 us
    all_to_all x1, starting transfers between devices, on_device(): lax.all_to_all(send_z, 'expert', 0, 0, tiled=True).reshape(slots, -1)  12.9 us
    ppermute x1, waiting for transfers between devices, on_device(): down = down + lax.ppermute(down, 'xh', swap)  12.9 us
    all_to_all x1, waiting for transfers between devices, on_device(): lax.all_to_all(pair_dx.reshape((2 * experts,) + pair_dx.shape[2:]), ('xh'...  11.8 us
    all_to_all x1, waiting for transfers between devices, on_device(): lax.all_to_all(send_z, 'expert', 0, 0, tiled=True).reshape(slots, -1)  11.6 us
    all_to_all x1, starting transfers between devices, on_device(): lax.all_to_all(pair_dx.reshape((2 * experts,) + pair_dx.shape[2:]), ('xh'...  11 us
    all_gather x1, waiting for transfers between devices, on_device(): downs = lax.all_gather(down, 'y', axis=0, tiled=False)  10.8 us
    unnamed x23, local copies, waits for them, and re-layouts  9.34 us
  transfers between devices with their start and end apart: 8, of which 6 were waited for; matrix products, arithmetic and copies ran while one was open for 7% of the time, Pallas kernels for 5%

profile of v3, /device:TPU:1, one launch (start us, length us, event | category | flops | bytes accessed | tf_op | source)
XLA Modules:
  0.0 157.6 jit_solution(10629795221994868159)
XLA Ops:
  7.2 0.0 copy-start
  7.2 1.0 copy.29
  8.2 0.7 reshape.84.tenant_ref
  8.9 0.7 copy-done.7
  9.6 0.7 copy-done.8
  10.3 2.0 %shard_map.112 = (bf16[1024,256]{1,0:T(8,128)(2,1)}, bf16[1024,384]{1,0:T(8,128)(2,1)S(1)}) custom-call(s32[2,384]{1,0:T(2,128)S(1)} %bitcast.79, bf16[2,384]{1,0:T(2,128)(2,1)S(1)} %bitcast.80, s32[1,384]{1,0:T(1,128)S(1)} %reshape.84.tenant_ref, bf16[192,768]{1,0:T(8,128)(2,1)S(1)} %bitcast.77), custom_call_target="tpu_custom_call" | custom-call | flops 402653184 | bytes 1572864 | tf_op jit(solution)/shard_map/pallas_call | solution.py:51
  12.3 12.9 %all-to-all-start = ((bf16[32,32,256]{2,1,0:T(8,128)(2,1)}), bf16[32,32,256]{2,1,0:T(8,128)(2,1)S(1)}, u32[]{:S(2)}, u32[]{:S(2)}) async-start(bf16[32,32,256]{2,1,0:T(8,128)(2,1)} %bitcast.5), calls=%async_computation | async-start | bytes 1048576 | tf_op jit(solution)/shard_map/all_to_all | solution.py:255
  25.2 0.0 all-gather.4.cloned.1.call-start
  25.3 0.0 copy-start.3
  25.3 0.5 convolution_convert_fusion
  25.8 1.2 copy.23
  27.0 1.5 copy-done.1
  28.5 0.6 shard_map.113
  29.2 1.0 copy-done.5
  30.2 11.6 %all-to-all-done = bf16[32,32,256]{2,1,0:T(8,128)(2,1)S(1)} async-done(((bf16[32,32,256]{2,1,0:T(8,128)(2,1)}), bf16[32,32,256]{2,1,0:T(8,128)(2,1)S(1)}, u32[]{:S(2)}, u32[]{:S(2)}) %all-to-all-start) | async-done | bytes 524320 | tf_op jit(solution)/shard_map/all_to_all | solution.py:255
  41.8 0.2 copy.25
  42.0 0.8 pad_maximum_fusion
  42.9 0.0 all-gather.4.cloned.1.call-update
  42.9 6.3 %all-to-all-start.1 = ((bf16[32,32,320]{2,1,0:T(8,128)(2,1)}), bf16[32,32,320]{2,1,0:T(8,128)(2,1)}, u32[]{:S(2)}, u32[]{:S(2)}) async-start(bf16[32,32,320]{2,1,0:T(8,128)(2,1)} %bitcast.83), calls=%async_computation.1 | async-start | bytes 1572864 | tf_op jit(solution)/shard_map/all_to_all | solution.py:270
  49.2 0.0 all-gather.6.cloned.1.call-start
  49.3 4.4 %collective-permute-start.1 = (bf16[2,320,896]{2,1,0:T(8,128)(2,1)S(1)}, bf16[2,320,896]{2,1,0:T(8,128)(2,1)}, u32[]{:S(2)}, u32[]{:S(2)}) collective-permute-start(bf16[2,320,896]{2,1,0:T(8,128)(2,1)S(1)} %get-tuple-element.31), channel_id=1, source_target_pairs={{0,256},{256,0},{1,257},{257,1},{2,258},{258,2},{3,259},{259,3},{4... | collective-permute-start | bytes 3440648 | tf_op jit(solution)/shard_map/ppermute | solution.py:262
  53.7 17.0 %all-to-all-done.1 = bf16[32,32,320]{2,1,0:T(8,128)(2,1)} async-done(((bf16[32,32,320]{2,1,0:T(8,128)(2,1)}), bf16[32,32,320]{2,1,0:T(8,128)(2,1)}, u32[]{:S(2)}, u32[]{:S(2)}) %all-to-all-start.1) | async-done | bytes 655392 | tf_op jit(solution)/shard_map/all_to_all | solution.py:270
  70.7 1.6 %fusion.3 = f32[1024,2,128]{0,2,1:T(8,128)S(1)} fusion(bf16[1024,320,1]{1,0,2:T(8,128)(2,1)} %bitcast.14, bf16[1,2,320,128]{3,2,1,0:T(8,128)(2,1)S(1)} %copy-done.3), kind=kOutput, calls=%fused_computation.24 | convolution fusion | flops 167772160 | bytes 1867776 | tf_op jit(solution)/shard_map/dot_general | solution.py:274
  72.3 0.1 select_reduce_fusion
  72.4 4.4 %collective-permute-start = (f32[32,1024]{1,0:T(8,128)S(1)}, f32[32,1024]{1,0:T(8,128)S(1)}, u32[]{:S(2)}, u32[]{:S(2)}) collective-permute-start(f32[32,1024]{1,0:T(8,128)S(1)} %bitcast.87), channel_id=1, source_target_pairs={{0,256},{256,0},{1,257},{257,1},{2,258},{258,2},{3,259},{259,3},{4... | collective-permute-start | bytes 393224 | tf_op jit(solution)/shard_map/ppermute | solution.py:280
  76.8 12.9 %collective-permute-done = f32[32,1024]{1,0:T(8,128)S(1)} collective-permute-done((f32[32,1024]{1,0:T(8,128)S(1)}, f32[32,1024]{1,0:T(8,128)S(1)}, u32[]{:S(2)}, u32[]{:S(2)}) %collective-permute-start) | collective-permute-done | bytes 131104 | tf_op jit(solution)/shard_map/ppermute | solution.py:280
  89.7 0.7 bitcast_add_fusion
  90.3 0.0 collective-permute-done.1.got_ref
  90.3 0.0 all-gather.6.cloned.1.call-update
  90.4 1.5 all-gather.4.cloned.1.call-done.z_ref
  91.9 2.0 %copy-done.4 = bf16[8,2,96,1152]{3,2,1,0:T(8,128)(2,1)S(1)} copy-done((bf16[8,2,96,1152]{3,2,1,0:T(8,128)(2,1)S(1)}, bf16[8,2,96,1152]{3,2,1,0:T(8,128)(2,1)}, u32[]{:S(2)}) %copy-start.4) | copy-done | bytes 3538968
  93.9 1.3 copy-done.6
  95.2 7.6 %shard_map.114 = (bf16[2,32,80,128]{3,2,1,0:T(8,128)(2,1)S(1)}, f32[32,1024]{1,0:T(8,128)S(1)}) custom-call(s32[1]{0:T(128)} %bitcast.2.half_ref, bf16[8,2,96,1152]{3,2,1,0:T(8,128)(2,1)S(1)} %copy-done.4, bf16[1024,256]{1,0:T(8,128)(2,1)S(1)} %bitcast.66, bf16[256,1024]{1,0:T(8,128)(2,1)S(1)} %bitcast.70, bf16[2,768,320]{2,1,0:T(8,128)(2,1)S(1)} %copy-done.6, ...), custom_call_target="tpu_custom_call" | custom-call | flops 2818572288 | bytes 6815744 | tf_op jit(solution)/shard_map/pallas_call | solution.py:162
  102.8 1.1 copy-done.2
  103.8 11.0 %all-to-all-start.2 = ((bf16[64,80,128]{2,1,0:T(8,128)(2,1)}), bf16[64,80,128]{2,1,0:T(8,128)(2,1)S(1)}, u32[]{:S(2)}, u32[]{:S(2)}) async-start(bf16[64,80,128]{2,1,0:T(8,128)(2,1)} %bitcast.74), calls=%async_computation.2 | async-start | bytes 2621440 | tf_op jit(solution)/shard_map/all_to_all | solution.py:288
  114.8 4.9 %collective-permute-start.2 = (f32[32,1024]{1,0:T(8,128)S(1)}, f32[32,1024]{1,0:T(8,128)S(1)}, u32[]{:S(2)}, u32[]{:S(2)}) collective-permute-start(f32[32,1024]{1,0:T(8,128)S(1)} %get-tuple-element.35), channel_id=1, source_target_pairs={{0,256},{256,0},{1,257},{257,1},{2,258},{258,2},{3,259},{259,3},{4... | collective-permute-start | bytes 393224 | tf_op jit(solution)/shard_map/ppermute | solution.py:292
  119.8 10.8 %all-gather.6.cloned.1.call-done = f32[256,1024]{1,0:T(8,128)} async-done(((f32[32,1024]{1,0:T(8,128)}), f32[256,1024]{1,0:T(8,128)}) %all-gather.6.cloned.1.call-update) | async-done | bytes 1048592 | tf_op jit(solution)/shard_map/all_gather | solution.py:282
  130.6 1.3 reduce_sum.19
  132.0 0.1 broadcast_in_dim.54
  132.2 0.1 broadcast_select_fusion
  132.3 0.2 convolution_bitcast_fusion.3
  132.5 0.2 convolution_bitcast_fusion.2
  132.7 0.7 pad_maximum_fusion.3
  133.4 1.5 convolution_bitcast_fusion.1
  134.9 1.5 convolution_bitcast_fusion
  136.5 0.7 pad_maximum_fusion.1
  137.2 11.8 %all-to-all-done.2 = bf16[64,80,128]{2,1,0:T(8,128)(2,1)S(1)} async-done(((bf16[64,80,128]{2,1,0:T(8,128)(2,1)}), bf16[64,80,128]{2,1,0:T(8,128)(2,1)S(1)}, u32[]{:S(2)}, u32[]{:S(2)}) %all-to-all-start.2) | async-done | bytes 1310752 | tf_op jit(solution)/shard_map/all_to_all | solution.py:288
  149.0 1.7 %shard_map.115 = bf16[320,384]{1,0:T(8,128)(2,1)} custom-call(bf16[2,32,80,128]{3,2,1,0:T(8,128)(2,1)S(1)} %bitcast.63, bf16[32,32,384]{2,1,0:T(8,128)(2,1)S(1)} %bitcast.64), custom_call_target="tpu_custom_call" | custom-call | flops 503316480 | bytes 2621440 | tf_op jit(solution)/shard_map/pallas_call | solution.py:210
  (23 shorter events, 0.2 us)
Async XLA Ops:
  7.2 18.1 %copy-start = (bf16[320,384]{1,0:T(8,128)(2,1)S(1)}, bf16[320,384]{1,0:T(8,128)(2,1)}, u32[]{:S(2)}) copy-start(bf16[320,384]{1,0:T(8,128)(2,1)} %param.10) | copy-start | bytes 737284
  7.2 18.1 %copy-start.10 = (bf16[1,2,5,1536]{3,1,2,0:T(2,128)(2,1)S(1)}, bf16[1,2,5,1536]{3,1,2,0:T(2,128)(2,1)}, u32[]{:S(2)}) copy-start(bf16[1,2,5,1536]{3,1,2,0:T(2,128)(2,1)} %param.15) | copy-start | bytes 92164
  8.9 0.7 copy-start.7
  9.6 0.7 copy-start.8
  12.3 29.5 %all-to-all-start = ((bf16[32,32,256]{2,1,0:T(8,128)(2,1)}), bf16[32,32,256]{2,1,0:T(8,128)(2,1)S(1)}, u32[]{:S(2)}, u32[]{:S(2)}) async-start(bf16[32,32,256]{2,1,0:T(8,128)(2,1)} %bitcast.5), calls=%async_computation | async-start | bytes 1048576 | tf_op jit(solution)/shard_map/all_to_all | solution.py:255
  25.2 66.7 %all-gather.4.cloned.1.call-start = ((), (), s32[]{:S(2)}) async-start(), calls=%async_computation.3 | async-start | bytes 3981312 | tf_op jit(solution)/shard_map/all_gather | solution.py:268
  25.3 1.7 %copy-start.3 = (bf16[1,2,320,128]{3,2,1,0:T(8,128)(2,1)S(1)}, bf16[1,2,320,128]{3,2,1,0:T(8,128)(2,1)}, u32[]{:S(2)}) copy-start(bf16[1,2,320,128]{3,2,1,0:T(8,128)(2,1)} %param.16) | copy-start | bytes 491524
  27.0 1.5 copy-start.1
  29.2 1.0 copy-start.5
  30.2 11.8 %copy-start.9 = (bf16[1,2,96,128]{3,2,1,0:T(8,128)(2,1)S(1)}, bf16[1,2,96,128]{3,2,1,0:T(8,128)(2,1)}, u32[]{:S(2)}) copy-start(bf16[1,2,96,128]{3,2,1,0:T(8,128)(2,1)} %param.17) | copy-start | bytes 147460
  42.9 27.8 %all-to-all-start.1 = ((bf16[32,32,320]{2,1,0:T(8,128)(2,1)}), bf16[32,32,320]{2,1,0:T(8,128)(2,1)}, u32[]{:S(2)}, u32[]{:S(2)}) async-start(bf16[32,32,320]{2,1,0:T(8,128)(2,1)} %bitcast.83), calls=%async_computation.1 | async-start | bytes 1572864 | tf_op jit(solution)/shard_map/all_to_all | solution.py:270
  49.2 81.4 %all-gather.6.cloned.1.call-start = ((), (), s32[]{:S(2)}) async-start(), calls=%async_computation.4 | async-start | bytes 1179648 | tf_op jit(solution)/shard_map/all_gather | solution.py:282
  49.3 41.0 %collective-permute-start.1 = (bf16[2,320,896]{2,1,0:T(8,128)(2,1)S(1)}, bf16[2,320,896]{2,1,0:T(8,128)(2,1)}, u32[]{:S(2)}, u32[]{:S(2)}) collective-permute-start(bf16[2,320,896]{2,1,0:T(8,128)(2,1)S(1)} %get-tuple-element.31), channel_id=1, source_target_pairs={{0,256},{256,0},{1,257},{257,1},{2,258},{258,2},{3,259},{259,3},{4... | collective-permute-start | bytes 3440648 | tf_op jit(solution)/shard_map/ppermute | solution.py:262
  72.4 17.2 %collective-permute-start = (f32[32,1024]{1,0:T(8,128)S(1)}, f32[32,1024]{1,0:T(8,128)S(1)}, u32[]{:S(2)}, u32[]{:S(2)}) collective-permute-start(f32[32,1024]{1,0:T(8,128)S(1)} %bitcast.87), channel_id=1, source_target_pairs={{0,256},{256,0},{1,257},{257,1},{2,258},{258,2},{3,259},{259,3},{4... | collective-permute-start | bytes 393224 | tf_op jit(solution)/shard_map/ppermute | solution.py:280
  91.9 2.0 %copy-start.4 = (bf16[8,2,96,1152]{3,2,1,0:T(8,128)(2,1)S(1)}, bf16[8,2,96,1152]{3,2,1,0:T(8,128)(2,1)}, u32[]{:S(2)}) copy-start(bf16[8,2,96,1152]{3,2,1,0:T(8,128)(2,1)} %all-gather.4.cloned.1.call-done.z_ref) | copy-start | bytes 10616836
  93.9 1.3 copy-start.6
  102.7 1.1 copy-start.2
  103.8 45.2 %all-to-all-start.2 = ((bf16[64,80,128]{2,1,0:T(8,128)(2,1)}), bf16[64,80,128]{2,1,0:T(8,128)(2,1)S(1)}, u32[]{:S(2)}, u32[]{:S(2)}) async-start(bf16[64,80,128]{2,1,0:T(8,128)(2,1)} %bitcast.74), calls=%async_computation.2 | async-start | bytes 2621440 | tf_op jit(solution)/shard_map/all_to_all | solution.py:288
  114.8 17.1 %collective-permute-start.2 = (f32[32,1024]{1,0:T(8,128)S(1)}, f32[32,1024]{1,0:T(8,128)S(1)}, u32[]{:S(2)}, u32[]{:S(2)}) collective-permute-start(f32[32,1024]{1,0:T(8,128)S(1)} %get-tuple-element.35), channel_id=1, source_target_pairs={{0,256},{256,0},{1,257},{257,1},{2,258},{258,2},{3,259},{259,3},{4... | collective-permute-start | bytes 393224 | tf_op jit(solution)/shard_map/ppermute | solution.py:292
Sparse Core Ops, SparseCore 0:
  43.0 48.8 all-gather.3
  94.6 35.9 all-gather.5

commit v4 on v3

--- a/solution.py
+++ b/solution.py
@@ -118,8 +118,8 @@
     half = half_ref[0]
     lane = lax.broadcasted_iota(jnp.int32, (tile, cols), 1)
 
-    def step(i, carry):
-        place = pl.ds(pl.multiple_of(i * tile, tile), tile)
+    def step(i):
+        place = pl.ds(i * tile, tile)
         gate = rows_ref[place, at : at + 1].astype(F32)
         tenant = rows_ref[place, at + 1 : at + 2].astype(F32)
         tenant_row = cols_ref[own + 1 : own + 2, place].astype(F32)
@@ -148,9 +148,9 @@
             rest = dx[:, :, full * 128 :]
             rest = jnp.concatenate([rest[:, : room // 2], rest[:, room // 2 :]], axis=2)
             dx_ref[where, from_experts, full * room :, :] = rest
-        return carry
-
-    lax.fori_loop(0, tiles, step, 0)
+
+    for i in range(tiles):
+        step(i)
 
 
 def pair_call(half, gathered, got_z, across_z, kept, got, first, rank, own, slots, experts):
@@ -176,7 +176,7 @@
             jax.ShapeDtypeStruct((planes * rank, slots), F32),
         ],
         scratch_shapes=[pltpu.VMEM((planes, depth, width), BF)],
-        compiler_params=pltpu.CompilerParams(vmem_limit_bytes=24 * 1024 * 1024),
+        compiler_params=pltpu.CompilerParams(vmem_limit_bytes=48 * 1024 * 1024),
         cost_estimate=pl.CostEstimate(
             flops=2 * slots * planes * depth * (2 * width + 2 * cols),
             bytes_accessed=2 * planes * depth * (wide + 2 * width) + 4 * slots * width,

time: 158 us -> 156 us (0.987)
  local copies, waits for them, and re-layouts: 11.6 us -> 9.57 us
    unnamed x23 -> x21, local copies, waits for them, and re-layouts: 9.34 us -> 7.33 us
where the time goes in v4:
time: 156 us
  waiting for transfers between devices  65.6 us (42%)
  starting transfers between devices  44 us (28%)
  between operations  14.3 us (9%)
  Pallas kernels  11.9 us (8%)
  local copies, waits for them, and re-layouts  9.57 us (6%)
  matrix products  5.68 us (4%)
  other arithmetic  4.53 us (3%)
    all_to_all x1, waiting for transfers between devices, on_device(): lax.all_to_all(send_x, 'expert', 0, 0, tiled=True)  17 us
    all_to_all x1, starting transfers between devices, on_device(): lax.all_to_all(send_z, 'expert', 0, 0, tiled=True).reshape(slots, -1)  12.9 us
    ppermute x1, waiting for transfers between devices, on_device(): down = down + lax.ppermute(down, 'xh', swap)  12.9 us
    all_gather x1, waiting for transfers between devices, on_device(): downs = lax.all_gather(down, 'y', axis=0, tiled=False)  12.2 us
    all_to_all x1, waiting for transfers between devices, on_device(): lax.all_to_all(send_z, 'expert', 0, 0, tiled=True).reshape(slots, -1)  11.6 us
    all_to_all x1, starting transfers between devices, on_device(): lax.all_to_all(pair_dx.reshape((2 * experts,) + pair_dx.shape[2:]), ('xh'...  11 us
    all_to_all x1, waiting for transfers between devices, on_device(): lax.all_to_all(pair_dx.reshape((2 * experts,) + pair_dx.shape[2:]), ('xh'...  10.4 us
    pallas_call x1, Pallas kernels, pair_call(): pl.pallas_call(functools.partial(pair_kernel, rank, tile, own), in_specs=...  7.55 us
  transfers between devices with their start and end apart: 8, of which 6 were waited for; matrix products, arithmetic and copies ran while one was open for 7% of the time, Pallas kernels for 5%

profile of v4, /device:TPU:1, one launch (start us, length us, event | category | flops | bytes accessed | tf_op | source)
XLA Modules:
  0.0 155.6 jit_solution(10712076067224793479)
XLA Ops:
  7.2 0.0 copy-start
  7.2 1.0 copy.29
  8.2 0.7 reshape.84.tenant_ref
  8.9 0.7 copy-done.6
  9.6 0.7 copy-done.7
  10.3 2.0 %shard_map.112 = (bf16[1024,256]{1,0:T(8,128)(2,1)}, bf16[1024,384]{1,0:T(8,128)(2,1)S(1)}) custom-call(s32[2,384]{1,0:T(2,128)S(1)} %bitcast.79, bf16[2,384]{1,0:T(2,128)(2,1)S(1)} %bitcast.80, s32[1,384]{1,0:T(1,128)S(1)} %reshape.84.tenant_ref, bf16[192,768]{1,0:T(8,128)(2,1)S(1)} %bitcast.77), custom_call_target="tpu_custom_call" | custom-call | flops 402653184 | bytes 1572864 | tf_op jit(solution)/shard_map/pallas_call | solution.py:51
  12.3 12.9 %all-to-all-start = ((bf16[32,32,256]{2,1,0:T(8,128)(2,1)}), bf16[32,32,256]{2,1,0:T(8,128)(2,1)S(1)}, u32[]{:S(2)}, u32[]{:S(2)}) async-start(bf16[32,32,256]{2,1,0:T(8,128)(2,1)} %bitcast.5), calls=%async_computation | async-start | bytes 1048576 | tf_op jit(solution)/shard_map/all_to_all | solution.py:255
  25.2 0.0 all-gather.4.cloned.1.call-start
  25.3 0.0 copy-start.3
  25.3 0.5 convolution_convert_fusion
  25.8 1.2 copy.23
  27.0 1.5 copy-done.1
  28.6 0.6 shard_map.113
  29.2 1.0 copy-done.4
  30.2 11.6 %all-to-all-done = bf16[32,32,256]{2,1,0:T(8,128)(2,1)S(1)} async-done(((bf16[32,32,256]{2,1,0:T(8,128)(2,1)}), bf16[32,32,256]{2,1,0:T(8,128)(2,1)S(1)}, u32[]{:S(2)}, u32[]{:S(2)}) %all-to-all-start) | async-done | bytes 524320 | tf_op jit(solution)/shard_map/all_to_all | solution.py:255
  41.8 0.2 copy.25
  42.0 0.8 pad_maximum_fusion
  42.9 0.0 all-gather.4.cloned.1.call-update
  42.9 6.3 %all-to-all-start.1 = ((bf16[32,32,320]{2,1,0:T(8,128)(2,1)}), bf16[32,32,320]{2,1,0:T(8,128)(2,1)}, u32[]{:S(2)}, u32[]{:S(2)}) async-start(bf16[32,32,320]{2,1,0:T(8,128)(2,1)} %bitcast.83), calls=%async_computation.1 | async-start | bytes 1572864 | tf_op jit(solution)/shard_map/all_to_all | solution.py:270
  49.2 0.0 all-gather.6.cloned.1.call-start
  49.3 4.4 %collective-permute-start.1 = (bf16[2,320,896]{2,1,0:T(8,128)(2,1)S(1)}, bf16[2,320,896]{2,1,0:T(8,128)(2,1)}, u32[]{:S(2)}, u32[]{:S(2)}) collective-permute-start(bf16[2,320,896]{2,1,0:T(8,128)(2,1)S(1)} %get-tuple-element.31), channel_id=1, source_target_pairs={{0,256},{256,0},{1,257},{257,1},{2,258},{258,2},{3,259},{259,3},{4... | collective-permute-start | bytes 3440648 | tf_op jit(solution)/shard_map/ppermute | solution.py:262
  53.7 17.0 %all-to-all-done.1 = bf16[32,32,320]{2,1,0:T(8,128)(2,1)} async-done(((bf16[32,32,320]{2,1,0:T(8,128)(2,1)}), bf16[32,32,320]{2,1,0:T(8,128)(2,1)}, u32[]{:S(2)}, u32[]{:S(2)}) %all-to-all-start.1) | async-done | bytes 655392 | tf_op jit(solution)/shard_map/all_to_all | solution.py:270
  70.7 1.6 %fusion.3 = f32[1024,2,128]{0,2,1:T(8,128)S(1)} fusion(bf16[1024,320,1]{1,0,2:T(8,128)(2,1)} %bitcast.14, bf16[1,2,320,128]{3,2,1,0:T(8,128)(2,1)S(1)} %copy-done.3), kind=kOutput, calls=%fused_computation.24 | convolution fusion | flops 167772160 | bytes 1867776 | tf_op jit(solution)/shard_map/dot_general | solution.py:274
  72.3 0.1 select_reduce_fusion
  72.4 4.4 %collective-permute-start = (f32[32,1024]{1,0:T(8,128)S(1)}, f32[32,1024]{1,0:T(8,128)S(1)}, u32[]{:S(2)}, u32[]{:S(2)}) collective-permute-start(f32[32,1024]{1,0:T(8,128)S(1)} %bitcast.87), channel_id=1, source_target_pairs={{0,256},{256,0},{1,257},{257,1},{2,258},{258,2},{3,259},{259,3},{4... | collective-permute-start | bytes 393224 | tf_op jit(solution)/shard_map/ppermute | solution.py:280
  76.8 12.9 %collective-permute-done = f32[32,1024]{1,0:T(8,128)S(1)} collective-permute-done((f32[32,1024]{1,0:T(8,128)S(1)}, f32[32,1024]{1,0:T(8,128)S(1)}, u32[]{:S(2)}, u32[]{:S(2)}) %collective-permute-start) | collective-permute-done | bytes 131104 | tf_op jit(solution)/shard_map/ppermute | solution.py:280
  89.7 0.7 bitcast_add_fusion
  90.3 0.0 collective-permute-done.1.got_ref
  90.3 0.0 all-gather.6.cloned.1.call-update
  90.4 1.5 all-gather.4.cloned.1.call-done.z_ref
  91.9 1.3 copy-done.5
  93.2 7.5 %shard_map.114 = (bf16[2,32,80,128]{3,2,1,0:T(8,128)(2,1)S(1)}, f32[32,1024]{1,0:T(8,128)S(1)}) custom-call(s32[1]{0:T(128)} %bitcast.2.half_ref, bf16[8,2,96,1152]{3,2,1,0:T(8,128)(2,1)} %all-gather.4.cloned.1.call-done.z_ref, bf16[1024,256]{1,0:T(8,128)(2,1)S(1)} %bitcast.66, bf16[256,1024]{1,0:T(8,128)(2,1)S(1)} %bitcast.70, ...), custom_call_target="tpu_custom_call" | custom-call | flops 2818572288 | bytes 6815744 | tf_op jit(solution)/shard_map/pallas_call | solution.py:162
  100.7 1.1 copy-done.2
  101.8 11.0 %all-to-all-start.2 = ((bf16[64,80,128]{2,1,0:T(8,128)(2,1)}), bf16[64,80,128]{2,1,0:T(8,128)(2,1)S(1)}, u32[]{:S(2)}, u32[]{:S(2)}) async-start(bf16[64,80,128]{2,1,0:T(8,128)(2,1)} %bitcast.74), calls=%async_computation.2 | async-start | bytes 2621440 | tf_op jit(solution)/shard_map/all_to_all | solution.py:288
  112.8 4.9 %collective-permute-start.2 = (f32[32,1024]{1,0:T(8,128)S(1)}, f32[32,1024]{1,0:T(8,128)S(1)}, u32[]{:S(2)}, u32[]{:S(2)}) collective-permute-start(f32[32,1024]{1,0:T(8,128)S(1)} %get-tuple-element.35), channel_id=1, source_target_pairs={{0,256},{256,0},{1,257},{257,1},{2,258},{258,2},{3,259},{259,3},{4... | collective-permute-start | bytes 393224 | tf_op jit(solution)/shard_map/ppermute | solution.py:292
  117.7 12.2 %all-gather.6.cloned.1.call-done = f32[256,1024]{1,0:T(8,128)} async-done(((f32[32,1024]{1,0:T(8,128)}), f32[256,1024]{1,0:T(8,128)}) %all-gather.6.cloned.1.call-update) | async-done | bytes 1048592 | tf_op jit(solution)/shard_map/all_gather | solution.py:282
  130.0 1.3 reduce_sum.19
  131.3 0.0 collective-permute-done.2
  131.3 0.1 broadcast_in_dim.54
  131.5 0.1 broadcast_select_fusion
  131.7 0.2 convolution_bitcast_fusion.3
  131.9 0.2 convolution_bitcast_fusion.2
  132.1 0.7 pad_maximum_fusion.3
  132.8 1.5 convolution_bitcast_fusion.1
  134.3 1.5 convolution_bitcast_fusion
  135.8 0.7 pad_maximum_fusion.1
  136.6 10.4 %all-to-all-done.2 = bf16[64,80,128]{2,1,0:T(8,128)(2,1)S(1)} async-done(((bf16[64,80,128]{2,1,0:T(8,128)(2,1)}), bf16[64,80,128]{2,1,0:T(8,128)(2,1)S(1)}, u32[]{:S(2)}, u32[]{:S(2)}) %all-to-all-start.2) | async-done | bytes 1310752 | tf_op jit(solution)/shard_map/all_to_all | solution.py:288
  147.0 1.7 %shard_map.115 = bf16[320,384]{1,0:T(8,128)(2,1)} custom-call(bf16[2,32,80,128]{3,2,1,0:T(8,128)(2,1)S(1)} %bitcast.63, bf16[32,32,384]{2,1,0:T(8,128)(2,1)S(1)} %bitcast.64), custom_call_target="tpu_custom_call" | custom-call | flops 503316480 | bytes 2621440 | tf_op jit(solution)/shard_map/pallas_call | solution.py:210
  (21 shorter events, 0.2 us)
Async XLA Ops:
  7.2 18.1 %copy-start = (bf16[320,384]{1,0:T(8,128)(2,1)S(1)}, bf16[320,384]{1,0:T(8,128)(2,1)}, u32[]{:S(2)}) copy-start(bf16[320,384]{1,0:T(8,128)(2,1)} %param.10) | copy-start | bytes 737284
  7.2 18.1 %copy-start.9 = (bf16[1,2,5,1536]{3,1,2,0:T(2,128)(2,1)S(1)}, bf16[1,2,5,1536]{3,1,2,0:T(2,128)(2,1)}, u32[]{:S(2)}) copy-start(bf16[1,2,5,1536]{3,1,2,0:T(2,128)(2,1)} %param.15) | copy-start | bytes 92164
  8.9 0.7 copy-start.6
  9.6 0.7 copy-start.7
  12.3 29.5 %all-to-all-start = ((bf16[32,32,256]{2,1,0:T(8,128)(2,1)}), bf16[32,32,256]{2,1,0:T(8,128)(2,1)S(1)}, u32[]{:S(2)}, u32[]{:S(2)}) async-start(bf16[32,32,256]{2,1,0:T(8,128)(2,1)} %bitcast.5), calls=%async_computation | async-start | bytes 1048576 | tf_op jit(solution)/shard_map/all_to_all | solution.py:255
  25.2 66.7 %all-gather.4.cloned.1.call-start = ((), (), s32[]{:S(2)}) async-start(), calls=%async_computation.3 | async-start | bytes 3981312 | tf_op jit(solution)/shard_map/all_gather | solution.py:268
  25.3 1.7 %copy-start.3 = (bf16[1,2,320,128]{3,2,1,0:T(8,128)(2,1)S(1)}, bf16[1,2,320,128]{3,2,1,0:T(8,128)(2,1)}, u32[]{:S(2)}) copy-start(bf16[1,2,320,128]{3,2,1,0:T(8,128)(2,1)} %param.16) | copy-start | bytes 491524
  27.0 1.5 copy-start.1
  29.2 1.0 copy-start.4
  30.2 11.8 %copy-start.8 = (bf16[1,2,96,128]{3,2,1,0:T(8,128)(2,1)S(1)}, bf16[1,2,96,128]{3,2,1,0:T(8,128)(2,1)}, u32[]{:S(2)}) copy-start(bf16[1,2,96,128]{3,2,1,0:T(8,128)(2,1)} %param.17) | copy-start | bytes 147460
  42.9 27.8 %all-to-all-start.1 = ((bf16[32,32,320]{2,1,0:T(8,128)(2,1)}), bf16[32,32,320]{2,1,0:T(8,128)(2,1)}, u32[]{:S(2)}, u32[]{:S(2)}) async-start(bf16[32,32,320]{2,1,0:T(8,128)(2,1)} %bitcast.83), calls=%async_computation.1 | async-start | bytes 1572864 | tf_op jit(solution)/shard_map/all_to_all | solution.py:270
  49.2 80.7 %all-gather.6.cloned.1.call-start = ((), (), s32[]{:S(2)}) async-start(), calls=%async_computation.4 | async-start | bytes 1179648 | tf_op jit(solution)/shard_map/all_gather | solution.py:282
  49.3 41.0 %collective-permute-start.1 = (bf16[2,320,896]{2,1,0:T(8,128)(2,1)S(1)}, bf16[2,320,896]{2,1,0:T(8,128)(2,1)}, u32[]{:S(2)}, u32[]{:S(2)}) collective-permute-start(bf16[2,320,896]{2,1,0:T(8,128)(2,1)S(1)} %get-tuple-element.31), channel_id=1, source_target_pairs={{0,256},{256,0},{1,257},{257,1},{2,258},{258,2},{3,259},{259,3},{4... | collective-permute-start | bytes 3440648 | tf_op jit(solution)/shard_map/ppermute | solution.py:262
  72.4 17.2 %collective-permute-start = (f32[32,1024]{1,0:T(8,128)S(1)}, f32[32,1024]{1,0:T(8,128)S(1)}, u32[]{:S(2)}, u32[]{:S(2)}) collective-permute-start(f32[32,1024]{1,0:T(8,128)S(1)} %bitcast.87), channel_id=1, source_target_pairs={{0,256},{256,0},{1,257},{257,1},{2,258},{258,2},{3,259},{259,3},{4... | collective-permute-start | bytes 393224 | tf_op jit(solution)/shard_map/ppermute | solution.py:280
  91.9 1.3 copy-start.5
  100.7 1.1 copy-start.2
  101.8 45.2 %all-to-all-start.2 = ((bf16[64,80,128]{2,1,0:T(8,128)(2,1)}), bf16[64,80,128]{2,1,0:T(8,128)(2,1)S(1)}, u32[]{:S(2)}, u32[]{:S(2)}) async-start(bf16[64,80,128]{2,1,0:T(8,128)(2,1)} %bitcast.74), calls=%async_computation.2 | async-start | bytes 2621440 | tf_op jit(solution)/shard_map/all_to_all | solution.py:288
  112.8 18.4 %collective-permute-start.2 = (f32[32,1024]{1,0:T(8,128)S(1)}, f32[32,1024]{1,0:T(8,128)S(1)}, u32[]{:S(2)}, u32[]{:S(2)}) collective-permute-start(f32[32,1024]{1,0:T(8,128)S(1)} %get-tuple-element.35), channel_id=1, source_target_pairs={{0,256},{256,0},{1,257},{257,1},{2,258},{258,2},{3,259},{259,3},{4... | collective-permute-start | bytes 393224 | tf_op jit(solution)/shard_map/ppermute | solution.py:292
Sparse Core Ops, SparseCore 0:
  43.0 48.8 all-gather.3
  94.6 35.3 all-gather.5

commit v5 on v4

--- a/solution.py
+++ b/solution.py
@@ -157,7 +157,7 @@
     ring, planes, hid, wide = gathered.shape
     cols = wide - slots
     depth, width = kept.shape[1:]
-    tile = 256 if slots % 256 == 0 else slots
+    tile = 512 if slots % 512 == 0 else slots
     vmem = pl.BlockSpec(memory_space=pltpu.VMEM)
     return pl.pallas_call(
         functools.partial(pair_kernel, rank, tile, own),

time: 156 us -> 156 us (level)
  no operation moved by 1% of the time
where the time goes in v5:
time: 156 us
  waiting for transfers between devices  65.6 us (42%)
  starting transfers between devices  43.9 us (28%)
  between operations  14.3 us (9%)
  Pallas kernels  11.8 us (8%)
  local copies, waits for them, and re-layouts  9.57 us (6%)
  matrix products  5.67 us (4%)
  other arithmetic  4.53 us (3%)
    all_to_all x1, waiting for transfers between devices, on_device(): lax.all_to_all(send_x, 'expert', 0, 0, tiled=True)  17 us
    all_to_all x1, starting transfers between devices, on_device(): lax.all_to_all(send_z, 'expert', 0, 0, tiled=True).reshape(slots, -1)  12.9 us
    ppermute x1, waiting for transfers between devices, on_device(): down = down + lax.ppermute(down, 'xh', swap)  12.9 us
    all_gather x1, waiting for transfers between devices, on_device(): downs = lax.all_gather(down, 'y', axis=0, tiled=False)  12.3 us
    all_to_all x1, waiting for transfers between devices, on_device(): lax.all_to_all(send_z, 'expert', 0, 0, tiled=True).reshape(slots, -1)  11.6 us
    all_to_all x1, starting transfers between devices, on_device(): lax.all_to_all(pair_dx.reshape((2 * experts,) + pair_dx.shape[2:]), ('xh'...  11 us
    all_to_all x1, waiting for transfers between devices, on_device(): lax.all_to_all(pair_dx.reshape((2 * experts,) + pair_dx.shape[2:]), ('xh'...  10.3 us
    pallas_call x1, Pallas kernels, pair_call(): pl.pallas_call(functools.partial(pair_kernel, rank, tile, own), in_specs=...  7.48 us
  transfers between devices with their start and end apart: 8, of which 6 were waited for; matrix products, arithmetic and copies ran while one was open for 7% of the time, Pallas kernels for 5%

profile of v5, /device:TPU:1, one launch (start us, length us, event | category | flops | bytes accessed | tf_op | source)
XLA Modules:
  0.0 155.5 jit_solution(15220994614448097534)
XLA Ops:
  7.2 0.0 copy-start
  7.2 1.0 copy.29
  8.2 0.7 reshape.84.tenant_ref
  8.9 0.7 copy-done.6
  9.6 0.7 copy-done.7
  10.3 2.0 %shard_map.112 = (bf16[1024,256]{1,0:T(8,128)(2,1)}, bf16[1024,384]{1,0:T(8,128)(2,1)S(1)}) custom-call(s32[2,384]{1,0:T(2,128)S(1)} %bitcast.79, bf16[2,384]{1,0:T(2,128)(2,1)S(1)} %bitcast.80, s32[1,384]{1,0:T(1,128)S(1)} %reshape.84.tenant_ref, bf16[192,768]{1,0:T(8,128)(2,1)S(1)} %bitcast.77), custom_call_target="tpu_custom_call" | custom-call | flops 402653184 | bytes 1572864 | tf_op jit(solution)/shard_map/pallas_call | solution.py:51
  12.3 12.9 %all-to-all-start = ((bf16[32,32,256]{2,1,0:T(8,128)(2,1)}), bf16[32,32,256]{2,1,0:T(8,128)(2,1)S(1)}, u32[]{:S(2)}, u32[]{:S(2)}) async-start(bf16[32,32,256]{2,1,0:T(8,128)(2,1)} %bitcast.5), calls=%async_computation | async-start | bytes 1048576 | tf_op jit(solution)/shard_map/all_to_all | solution.py:255
  25.2 0.0 all-gather.4.cloned.1.call-start
  25.3 0.0 copy-start.3
  25.3 0.5 convolution_convert_fusion
  25.8 1.2 copy.23
  27.0 1.5 copy-done.1
  28.6 0.6 shard_map.113
  29.2 1.0 copy-done.4
  30.2 11.6 %all-to-all-done = bf16[32,32,256]{2,1,0:T(8,128)(2,1)S(1)} async-done(((bf16[32,32,256]{2,1,0:T(8,128)(2,1)}), bf16[32,32,256]{2,1,0:T(8,128)(2,1)S(1)}, u32[]{:S(2)}, u32[]{:S(2)}) %all-to-all-start) | async-done | bytes 524320 | tf_op jit(solution)/shard_map/all_to_all | solution.py:255
  41.8 0.2 copy.25
  42.0 0.8 pad_maximum_fusion
  42.9 0.0 all-gather.4.cloned.1.call-update
  42.9 6.3 %all-to-all-start.1 = ((bf16[32,32,320]{2,1,0:T(8,128)(2,1)}), bf16[32,32,320]{2,1,0:T(8,128)(2,1)}, u32[]{:S(2)}, u32[]{:S(2)}) async-start(bf16[32,32,320]{2,1,0:T(8,128)(2,1)} %bitcast.83), calls=%async_computation.1 | async-start | bytes 1572864 | tf_op jit(solution)/shard_map/all_to_all | solution.py:270
  49.2 0.0 all-gather.6.cloned.1.call-start
  49.3 4.4 %collective-permute-start.1 = (bf16[2,320,896]{2,1,0:T(8,128)(2,1)S(1)}, bf16[2,320,896]{2,1,0:T(8,128)(2,1)}, u32[]{:S(2)}, u32[]{:S(2)}) collective-permute-start(bf16[2,320,896]{2,1,0:T(8,128)(2,1)S(1)} %get-tuple-element.31), channel_id=1, source_target_pairs={{0,256},{256,0},{1,257},{257,1},{2,258},{258,2},{3,259},{259,3},{4... | collective-permute-start | bytes 3440648 | tf_op jit(solution)/shard_map/ppermute | solution.py:262
  53.7 17.0 %all-to-all-done.1 = bf16[32,32,320]{2,1,0:T(8,128)(2,1)} async-done(((bf16[32,32,320]{2,1,0:T(8,128)(2,1)}), bf16[32,32,320]{2,1,0:T(8,128)(2,1)}, u32[]{:S(2)}, u32[]{:S(2)}) %all-to-all-start.1) | async-done | bytes 655392 | tf_op jit(solution)/shard_map/all_to_all | solution.py:270
  70.7 1.6 %fusion.3 = f32[1024,2,128]{0,2,1:T(8,128)S(1)} fusion(bf16[1024,320,1]{1,0,2:T(8,128)(2,1)} %bitcast.14, bf16[1,2,320,128]{3,2,1,0:T(8,128)(2,1)S(1)} %copy-done.3), kind=kOutput, calls=%fused_computation.24 | convolution fusion | flops 167772160 | bytes 1867776 | tf_op jit(solution)/shard_map/dot_general | solution.py:274
  72.3 0.1 select_reduce_fusion
  72.4 4.4 %collective-permute-start = (f32[32,1024]{1,0:T(8,128)S(1)}, f32[32,1024]{1,0:T(8,128)S(1)}, u32[]{:S(2)}, u32[]{:S(2)}) collective-permute-start(f32[32,1024]{1,0:T(8,128)S(1)} %bitcast.87), channel_id=1, source_target_pairs={{0,256},{256,0},{1,257},{257,1},{2,258},{258,2},{3,259},{259,3},{4... | collective-permute-start | bytes 393224 | tf_op jit(solution)/shard_map/ppermute | solution.py:280
  76.8 12.9 %collective-permute-done = f32[32,1024]{1,0:T(8,128)S(1)} collective-permute-done((f32[32,1024]{1,0:T(8,128)S(1)}, f32[32,1024]{1,0:T(8,128)S(1)}, u32[]{:S(2)}, u32[]{:S(2)}) %collective-permute-start) | collective-permute-done | bytes 131104 | tf_op jit(solution)/shard_map/ppermute | solution.py:280
  89.7 0.7 bitcast_add_fusion
  90.3 0.0 collective-permute-done.1.got_ref
  90.3 0.0 all-gather.6.cloned.1.call-update
  90.4 1.5 all-gather.4.cloned.1.call-done.z_ref
  91.9 1.3 copy-done.5
  93.2 7.5 %shard_map.114 = (bf16[2,32,80,128]{3,2,1,0:T(8,128)(2,1)S(1)}, f32[32,1024]{1,0:T(8,128)S(1)}) custom-call(s32[1]{0:T(128)} %bitcast.2.half_ref, bf16[8,2,96,1152]{3,2,1,0:T(8,128)(2,1)} %all-gather.4.cloned.1.call-done.z_ref, bf16[1024,256]{1,0:T(8,128)(2,1)S(1)} %bitcast.66, bf16[256,1024]{1,0:T(8,128)(2,1)S(1)} %bitcast.70, ...), custom_call_target="tpu_custom_call" | custom-call | flops 2818572288 | bytes 6815744 | tf_op jit(solution)/shard_map/pallas_call | solution.py:162
  100.7 1.1 copy-done.2
  101.7 11.0 %all-to-all-start.2 = ((bf16[64,80,128]{2,1,0:T(8,128)(2,1)}), bf16[64,80,128]{2,1,0:T(8,128)(2,1)S(1)}, u32[]{:S(2)}, u32[]{:S(2)}) async-start(bf16[64,80,128]{2,1,0:T(8,128)(2,1)} %bitcast.74), calls=%async_computation.2 | async-start | bytes 2621440 | tf_op jit(solution)/shard_map/all_to_all | solution.py:288
  112.8 4.9 %collective-permute-start.2 = (f32[32,1024]{1,0:T(8,128)S(1)}, f32[32,1024]{1,0:T(8,128)S(1)}, u32[]{:S(2)}, u32[]{:S(2)}) collective-permute-start(f32[32,1024]{1,0:T(8,128)S(1)} %get-tuple-element.35), channel_id=1, source_target_pairs={{0,256},{256,0},{1,257},{257,1},{2,258},{258,2},{3,259},{259,3},{4... | collective-permute-start | bytes 393224 | tf_op jit(solution)/shard_map/ppermute | solution.py:292
  117.7 12.3 %all-gather.6.cloned.1.call-done = f32[256,1024]{1,0:T(8,128)} async-done(((f32[32,1024]{1,0:T(8,128)}), f32[256,1024]{1,0:T(8,128)}) %all-gather.6.cloned.1.call-update) | async-done | bytes 1048592 | tf_op jit(solution)/shard_map/all_gather | solution.py:282
  130.0 1.3 reduce_sum.19
  131.3 0.0 collective-permute-done.2
  131.3 0.1 broadcast_in_dim.54
  131.5 0.1 broadcast_select_fusion
  131.7 0.2 convolution_bitcast_fusion.3
  131.9 0.2 convolution_bitcast_fusion.2
  132.1 0.7 pad_maximum_fusion.3
  132.8 1.5 convolution_bitcast_fusion.1
  134.3 1.5 convolution_bitcast_fusion
  135.8 0.7 pad_maximum_fusion.1
  136.6 10.3 %all-to-all-done.2 = bf16[64,80,128]{2,1,0:T(8,128)(2,1)S(1)} async-done(((bf16[64,80,128]{2,1,0:T(8,128)(2,1)}), bf16[64,80,128]{2,1,0:T(8,128)(2,1)S(1)}, u32[]{:S(2)}, u32[]{:S(2)}) %all-to-all-start.2) | async-done | bytes 1310752 | tf_op jit(solution)/shard_map/all_to_all | solution.py:288
  146.9 1.7 %shard_map.115 = bf16[320,384]{1,0:T(8,128)(2,1)} custom-call(bf16[2,32,80,128]{3,2,1,0:T(8,128)(2,1)S(1)} %bitcast.63, bf16[32,32,384]{2,1,0:T(8,128)(2,1)S(1)} %bitcast.64), custom_call_target="tpu_custom_call" | custom-call | flops 503316480 | bytes 2621440 | tf_op jit(solution)/shard_map/pallas_call | solution.py:210
  (21 shorter events, 0.2 us)
Async XLA Ops:
  7.2 18.1 %copy-start = (bf16[320,384]{1,0:T(8,128)(2,1)S(1)}, bf16[320,384]{1,0:T(8,128)(2,1)}, u32[]{:S(2)}) copy-start(bf16[320,384]{1,0:T(8,128)(2,1)} %param.10) | copy-start | bytes 737284
  7.2 18.1 %copy-start.9 = (bf16[1,2,5,1536]{3,1,2,0:T(2,128)(2,1)S(1)}, bf16[1,2,5,1536]{3,1,2,0:T(2,128)(2,1)}, u32[]{:S(2)}) copy-start(bf16[1,2,5,1536]{3,1,2,0:T(2,128)(2,1)} %param.15) | copy-start | bytes 92164
  8.9 0.7 copy-start.6
  9.6 0.7 copy-start.7
  12.3 29.5 %all-to-all-start = ((bf16[32,32,256]{2,1,0:T(8,128)(2,1)}), bf16[32,32,256]{2,1,0:T(8,128)(2,1)S(1)}, u32[]{:S(2)}, u32[]{:S(2)}) async-start(bf16[32,32,256]{2,1,0:T(8,128)(2,1)} %bitcast.5), calls=%async_computation | async-start | bytes 1048576 | tf_op jit(solution)/shard_map/all_to_all | solution.py:255
  25.2 66.7 %all-gather.4.cloned.1.call-start = ((), (), s32[]{:S(2)}) async-start(), calls=%async_computation.3 | async-start | bytes 3981312 | tf_op jit(solution)/shard_map/all_gather | solution.py:268
  25.3 1.7 %copy-start.3 = (bf16[1,2,320,128]{3,2,1,0:T(8,128)(2,1)S(1)}, bf16[1,2,320,128]{3,2,1,0:T(8,128)(2,1)}, u32[]{:S(2)}) copy-start(bf16[1,2,320,128]{3,2,1,0:T(8,128)(2,1)} %param.16) | copy-start | bytes 491524
  27.0 1.5 copy-start.1
  29.2 1.0 copy-start.4
  30.2 11.8 %copy-start.8 = (bf16[1,2,96,128]{3,2,1,0:T(8,128)(2,1)S(1)}, bf16[1,2,96,128]{3,2,1,0:T(8,128)(2,1)}, u32[]{:S(2)}) copy-start(bf16[1,2,96,128]{3,2,1,0:T(8,128)(2,1)} %param.17) | copy-start | bytes 147460
  42.9 27.8 %all-to-all-start.1 = ((bf16[32,32,320]{2,1,0:T(8,128)(2,1)}), bf16[32,32,320]{2,1,0:T(8,128)(2,1)}, u32[]{:S(2)}, u32[]{:S(2)}) async-start(bf16[32,32,320]{2,1,0:T(8,128)(2,1)} %bitcast.83), calls=%async_computation.1 | async-start | bytes 1572864 | tf_op jit(solution)/shard_map/all_to_all | solution.py:270
  49.2 80.7 %all-gather.6.cloned.1.call-start = ((), (), s32[]{:S(2)}) async-start(), calls=%async_computation.4 | async-start | bytes 1179648 | tf_op jit(solution)/shard_map/all_gather | solution.py:282
  49.3 41.0 %collective-permute-start.1 = (bf16[2,320,896]{2,1,0:T(8,128)(2,1)S(1)}, bf16[2,320,896]{2,1,0:T(8,128)(2,1)}, u32[]{:S(2)}, u32[]{:S(2)}) collective-permute-start(bf16[2,320,896]{2,1,0:T(8,128)(2,1)S(1)} %get-tuple-element.31), channel_id=1, source_target_pairs={{0,256},{256,0},{1,257},{257,1},{2,258},{258,2},{3,259},{259,3},{4... | collective-permute-start | bytes 3440648 | tf_op jit(solution)/shard_map/ppermute | solution.py:262
  72.4 17.2 %collective-permute-start = (f32[32,1024]{1,0:T(8,128)S(1)}, f32[32,1024]{1,0:T(8,128)S(1)}, u32[]{:S(2)}, u32[]{:S(2)}) collective-permute-start(f32[32,1024]{1,0:T(8,128)S(1)} %bitcast.87), channel_id=1, source_target_pairs={{0,256},{256,0},{1,257},{257,1},{2,258},{258,2},{3,259},{259,3},{4... | collective-permute-start | bytes 393224 | tf_op jit(solution)/shard_map/ppermute | solution.py:280
  91.9 1.3 copy-start.5
  100.7 1.1 copy-start.2
  101.7 45.2 %all-to-all-start.2 = ((bf16[64,80,128]{2,1,0:T(8,128)(2,1)}), bf16[64,80,128]{2,1,0:T(8,128)(2,1)S(1)}, u32[]{:S(2)}, u32[]{:S(2)}) async-start(bf16[64,80,128]{2,1,0:T(8,128)(2,1)} %bitcast.74), calls=%async_computation.2 | async-start | bytes 2621440 | tf_op jit(solution)/shard_map/all_to_all | solution.py:288
  112.8 18.5 %collective-permute-start.2 = (f32[32,1024]{1,0:T(8,128)S(1)}, f32[32,1024]{1,0:T(8,128)S(1)}, u32[]{:S(2)}, u32[]{:S(2)}) collective-permute-start(f32[32,1024]{1,0:T(8,128)S(1)} %get-tuple-element.35), channel_id=1, source_target_pairs={{0,256},{256,0},{1,257},{257,1},{2,258},{258,2},{3,259},{259,3},{4... | collective-permute-start | bytes 393224 | tf_op jit(solution)/shard_map/ppermute | solution.py:292
Sparse Core Ops, SparseCore 0:
  43.0 48.8 all-gather.3
  94.6 35.3 all-gather.5

commit v6 on v5

--- a/solution.py
+++ b/solution.py
@@ -157,7 +157,7 @@
     ring, planes, hid, wide = gathered.shape
     cols = wide - slots
     depth, width = kept.shape[1:]
-    tile = 512 if slots % 512 == 0 else slots
+    tile = slots
     vmem = pl.BlockSpec(memory_space=pltpu.VMEM)
     return pl.pallas_call(
         functools.partial(pair_kernel, rank, tile, own),

time: 156 us -> 156 us (level)
  no operation moved by 1% of the time
where the time goes in v6:
time: 156 us; the launch traced here: 155 us
  waiting for transfers between devices  65.6 us (42%)
  starting transfers between devices  43.9 us (28%)
  between operations  14.3 us (9%)
  Pallas kernels  11.8 us (8%)
  local copies, waits for them, and re-layouts  9.57 us (6%)
  matrix products  5.68 us (4%)
  other arithmetic  4.53 us (3%)
    all_to_all x1, waiting for transfers between devices, on_device(): lax.all_to_all(send_x, 'expert', 0, 0, tiled=True)  17 us
    all_to_all x1, starting transfers between devices, on_device(): lax.all_to_all(send_z, 'expert', 0, 0, tiled=True).reshape(slots, -1)  12.9 us
    ppermute x1, waiting for transfers between devices, on_device(): down = down + lax.ppermute(down, 'xh', swap)  12.9 us
    all_gather x1, waiting for transfers between devices, on_device(): downs = lax.all_gather(down, 'y', axis=0, tiled=False)  12.3 us
    all_to_all x1, waiting for transfers between devices, on_device(): lax.all_to_all(send_z, 'expert', 0, 0, tiled=True).reshape(slots, -1)  11.6 us
    all_to_all x1, starting transfers between devices, on_device(): lax.all_to_all(pair_dx.reshape((2 * experts,) + pair_dx.shape[2:]), ('xh'...  11 us
    all_to_all x1, waiting for transfers between devices, on_device(): lax.all_to_all(pair_dx.reshape((2 * experts,) + pair_dx.shape[2:]), ('xh'...  10.3 us
    pallas_call x1, Pallas kernels, pair_call(): pl.pallas_call(functools.partial(pair_kernel, rank, tile, own), in_specs=...  7.47 us
  transfers between devices with their start and end apart: 8, of which 6 were waited for; matrix products, arithmetic and copies ran while one was open for 7% of the time, Pallas kernels for 5%

profile of v6, /device:TPU:1, one launch (start us, length us, event | category | flops | bytes accessed | tf_op | source)
XLA Modules:
  0.0 155.5 jit_solution(3629733555668440825)
XLA Ops:
  7.2 0.0 copy-start
  7.2 1.0 copy.29
  8.2 0.7 reshape.84.tenant_ref
  8.9 0.7 copy-done.6
  9.6 0.7 copy-done.7
  10.3 2.0 %shard_map.112 = (bf16[1024,256]{1,0:T(8,128)(2,1)}, bf16[1024,384]{1,0:T(8,128)(2,1)S(1)}) custom-call(s32[2,384]{1,0:T(2,128)S(1)} %bitcast.79, bf16[2,384]{1,0:T(2,128)(2,1)S(1)} %bitcast.80, s32[1,384]{1,0:T(1,128)S(1)} %reshape.84.tenant_ref, bf16[192,768]{1,0:T(8,128)(2,1)S(1)} %bitcast.77), custom_call_target="tpu_custom_call" | custom-call | flops 402653184 | bytes 1572864 | tf_op jit(solution)/shard_map/pallas_call | solution.py:51
  12.3 12.9 %all-to-all-start = ((bf16[32,32,256]{2,1,0:T(8,128)(2,1)}), bf16[32,32,256]{2,1,0:T(8,128)(2,1)S(1)}, u32[]{:S(2)}, u32[]{:S(2)}) async-start(bf16[32,32,256]{2,1,0:T(8,128)(2,1)} %bitcast.5), calls=%async_computation | async-start | bytes 1048576 | tf_op jit(solution)/shard_map/all_to_all | solution.py:255
  25.2 0.0 all-gather.4.cloned.1.call-start
  25.3 0.0 copy-start.3
  25.3 0.5 convolution_convert_fusion
  25.8 1.2 copy.23
  27.0 1.5 copy-done.1
  28.6 0.6 shard_map.113
  29.2 1.0 copy-done.4
  30.2 11.6 %all-to-all-done = bf16[32,32,256]{2,1,0:T(8,128)(2,1)S(1)} async-done(((bf16[32,32,256]{2,1,0:T(8,128)(2,1)}), bf16[32,32,256]{2,1,0:T(8,128)(2,1)S(1)}, u32[]{:S(2)}, u32[]{:S(2)}) %all-to-all-start) | async-done | bytes 524320 | tf_op jit(solution)/shard_map/all_to_all | solution.py:255
  41.8 0.2 copy.25
  42.0 0.8 pad_maximum_fusion
  42.9 0.0 all-gather.4.cloned.1.call-update
  42.9 6.3 %all-to-all-start.1 = ((bf16[32,32,320]{2,1,0:T(8,128)(2,1)}), bf16[32,32,320]{2,1,0:T(8,128)(2,1)}, u32[]{:S(2)}, u32[]{:S(2)}) async-start(bf16[32,32,320]{2,1,0:T(8,128)(2,1)} %bitcast.83), calls=%async_computation.1 | async-start | bytes 1572864 | tf_op jit(solution)/shard_map/all_to_all | solution.py:270
  49.2 0.0 all-gather.6.cloned.1.call-start
  49.3 4.4 %collective-permute-start.1 = (bf16[2,320,896]{2,1,0:T(8,128)(2,1)S(1)}, bf16[2,320,896]{2,1,0:T(8,128)(2,1)}, u32[]{:S(2)}, u32[]{:S(2)}) collective-permute-start(bf16[2,320,896]{2,1,0:T(8,128)(2,1)S(1)} %get-tuple-element.31), channel_id=1, source_target_pairs={{0,256},{256,0},{1,257},{257,1},{2,258},{258,2},{3,259},{259,3},{4... | collective-permute-start | bytes 3440648 | tf_op jit(solution)/shard_map/ppermute | solution.py:262
  53.7 17.0 %all-to-all-done.1 = bf16[32,32,320]{2,1,0:T(8,128)(2,1)} async-done(((bf16[32,32,320]{2,1,0:T(8,128)(2,1)}), bf16[32,32,320]{2,1,0:T(8,128)(2,1)}, u32[]{:S(2)}, u32[]{:S(2)}) %all-to-all-start.1) | async-done | bytes 655392 | tf_op jit(solution)/shard_map/all_to_all | solution.py:270
  70.7 1.6 %fusion.3 = f32[1024,2,128]{0,2,1:T(8,128)S(1)} fusion(bf16[1024,320,1]{1,0,2:T(8,128)(2,1)} %bitcast.14, bf16[1,2,320,128]{3,2,1,0:T(8,128)(2,1)S(1)} %copy-done.3), kind=kOutput, calls=%fused_computation.24 | convolution fusion | flops 167772160 | bytes 1867776 | tf_op jit(solution)/shard_map/dot_general | solution.py:274
  72.3 0.1 select_reduce_fusion
  72.4 4.4 %collective-permute-start = (f32[32,1024]{1,0:T(8,128)S(1)}, f32[32,1024]{1,0:T(8,128)S(1)}, u32[]{:S(2)}, u32[]{:S(2)}) collective-permute-start(f32[32,1024]{1,0:T(8,128)S(1)} %bitcast.87), channel_id=1, source_target_pairs={{0,256},{256,0},{1,257},{257,1},{2,258},{258,2},{3,259},{259,3},{4... | collective-permute-start | bytes 393224 | tf_op jit(solution)/shard_map/ppermute | solution.py:280
  76.8 12.9 %collective-permute-done = f32[32,1024]{1,0:T(8,128)S(1)} collective-permute-done((f32[32,1024]{1,0:T(8,128)S(1)}, f32[32,1024]{1,0:T(8,128)S(1)}, u32[]{:S(2)}, u32[]{:S(2)}) %collective-permute-start) | collective-permute-done | bytes 131104 | tf_op jit(solution)/shard_map/ppermute | solution.py:280
  89.7 0.7 bitcast_add_fusion
  90.3 0.0 collective-permute-done.1.got_ref
  90.3 0.0 all-gather.6.cloned.1.call-update
  90.4 1.5 all-gather.4.cloned.1.call-done.z_ref
  91.9 1.3 copy-done.5
  93.2 7.5 %shard_map.114 = (bf16[2,32,80,128]{3,2,1,0:T(8,128)(2,1)S(1)}, f32[32,1024]{1,0:T(8,128)S(1)}) custom-call(s32[1]{0:T(128)} %bitcast.2.half_ref, bf16[8,2,96,1152]{3,2,1,0:T(8,128)(2,1)} %all-gather.4.cloned.1.call-done.z_ref, bf16[1024,256]{1,0:T(8,128)(2,1)S(1)} %bitcast.66, bf16[256,1024]{1,0:T(8,128)(2,1)S(1)} %bitcast.70, ...), custom_call_target="tpu_custom_call" | custom-call | flops 2818572288 | bytes 6815744 | tf_op jit(solution)/shard_map/pallas_call | solution.py:162
  100.7 1.1 copy-done.2
  101.7 11.0 %all-to-all-start.2 = ((bf16[64,80,128]{2,1,0:T(8,128)(2,1)}), bf16[64,80,128]{2,1,0:T(8,128)(2,1)S(1)}, u32[]{:S(2)}, u32[]{:S(2)}) async-start(bf16[64,80,128]{2,1,0:T(8,128)(2,1)} %bitcast.74), calls=%async_computation.2 | async-start | bytes 2621440 | tf_op jit(solution)/shard_map/all_to_all | solution.py:288
  112.7 4.9 %collective-permute-start.2 = (f32[32,1024]{1,0:T(8,128)S(1)}, f32[32,1024]{1,0:T(8,128)S(1)}, u32[]{:S(2)}, u32[]{:S(2)}) collective-permute-start(f32[32,1024]{1,0:T(8,128)S(1)} %get-tuple-element.35), channel_id=1, source_target_pairs={{0,256},{256,0},{1,257},{257,1},{2,258},{258,2},{3,259},{259,3},{4... | collective-permute-start | bytes 393224 | tf_op jit(solution)/shard_map/ppermute | solution.py:292
  117.7 12.3 %all-gather.6.cloned.1.call-done = f32[256,1024]{1,0:T(8,128)} async-done(((f32[32,1024]{1,0:T(8,128)}), f32[256,1024]{1,0:T(8,128)}) %all-gather.6.cloned.1.call-update) | async-done | bytes 1048592 | tf_op jit(solution)/shard_map/all_gather | solution.py:282
  130.0 1.3 reduce_sum.19
  131.3 0.0 collective-permute-done.2
  131.3 0.1 broadcast_in_dim.54
  131.5 0.1 broadcast_select_fusion
  131.7 0.2 convolution_bitcast_fusion.3
  131.9 0.2 convolution_bitcast_fusion.2
  132.1 0.7 pad_maximum_fusion.3
  132.8 1.5 convolution_bitcast_fusion.1
  134.3 1.5 convolution_bitcast_fusion
  135.8 0.7 pad_maximum_fusion.1
  136.6 10.3 %all-to-all-done.2 = bf16[64,80,128]{2,1,0:T(8,128)(2,1)S(1)} async-done(((bf16[64,80,128]{2,1,0:T(8,128)(2,1)}), bf16[64,80,128]{2,1,0:T(8,128)(2,1)S(1)}, u32[]{:S(2)}, u32[]{:S(2)}) %all-to-all-start.2) | async-done | bytes 1310752 | tf_op jit(solution)/shard_map/all_to_all | solution.py:288
  146.9 1.7 %shard_map.115 = bf16[320,384]{1,0:T(8,128)(2,1)} custom-call(bf16[2,32,80,128]{3,2,1,0:T(8,128)(2,1)S(1)} %bitcast.63, bf16[32,32,384]{2,1,0:T(8,128)(2,1)S(1)} %bitcast.64), custom_call_target="tpu_custom_call" | custom-call | flops 503316480 | bytes 2621440 | tf_op jit(solution)/shard_map/pallas_call | solution.py:210
  (21 shorter events, 0.2 us)
Async XLA Ops:
  7.2 18.1 %copy-start = (bf16[320,384]{1,0:T(8,128)(2,1)S(1)}, bf16[320,384]{1,0:T(8,128)(2,1)}, u32[]{:S(2)}) copy-start(bf16[320,384]{1,0:T(8,128)(2,1)} %param.10) | copy-start | bytes 737284
  7.2 18.1 %copy-start.9 = (bf16[1,2,5,1536]{3,1,2,0:T(2,128)(2,1)S(1)}, bf16[1,2,5,1536]{3,1,2,0:T(2,128)(2,1)}, u32[]{:S(2)}) copy-start(bf16[1,2,5,1536]{3,1,2,0:T(2,128)(2,1)} %param.15) | copy-start | bytes 92164
  8.9 0.7 copy-start.6
  9.6 0.7 copy-start.7
  12.3 29.5 %all-to-all-start = ((bf16[32,32,256]{2,1,0:T(8,128)(2,1)}), bf16[32,32,256]{2,1,0:T(8,128)(2,1)S(1)}, u32[]{:S(2)}, u32[]{:S(2)}) async-start(bf16[32,32,256]{2,1,0:T(8,128)(2,1)} %bitcast.5), calls=%async_computation | async-start | bytes 1048576 | tf_op jit(solution)/shard_map/all_to_all | solution.py:255
  25.2 66.7 %all-gather.4.cloned.1.call-start = ((), (), s32[]{:S(2)}) async-start(), calls=%async_computation.3 | async-start | bytes 3981312 | tf_op jit(solution)/shard_map/all_gather | solution.py:268
  25.3 1.7 %copy-start.3 = (bf16[1,2,320,128]{3,2,1,0:T(8,128)(2,1)S(1)}, bf16[1,2,320,128]{3,2,1,0:T(8,128)(2,1)}, u32[]{:S(2)}) copy-start(bf16[1,2,320,128]{3,2,1,0:T(8,128)(2,1)} %param.16) | copy-start | bytes 491524
  27.0 1.5 copy-start.1
  29.2 1.0 copy-start.4
  30.2 11.8 %copy-start.8 = (bf16[1,2,96,128]{3,2,1,0:T(8,128)(2,1)S(1)}, bf16[1,2,96,128]{3,2,1,0:T(8,128)(2,1)}, u32[]{:S(2)}) copy-start(bf16[1,2,96,128]{3,2,1,0:T(8,128)(2,1)} %param.17) | copy-start | bytes 147460
  42.9 27.8 %all-to-all-start.1 = ((bf16[32,32,320]{2,1,0:T(8,128)(2,1)}), bf16[32,32,320]{2,1,0:T(8,128)(2,1)}, u32[]{:S(2)}, u32[]{:S(2)}) async-start(bf16[32,32,320]{2,1,0:T(8,128)(2,1)} %bitcast.83), calls=%async_computation.1 | async-start | bytes 1572864 | tf_op jit(solution)/shard_map/all_to_all | solution.py:270
  49.2 80.7 %all-gather.6.cloned.1.call-start = ((), (), s32[]{:S(2)}) async-start(), calls=%async_computation.4 | async-start | bytes 1179648 | tf_op jit(solution)/shard_map/all_gather | solution.py:282
  49.3 41.0 %collective-permute-start.1 = (bf16[2,320,896]{2,1,0:T(8,128)(2,1)S(1)}, bf16[2,320,896]{2,1,0:T(8,128)(2,1)}, u32[]{:S(2)}, u32[]{:S(2)}) collective-permute-start(bf16[2,320,896]{2,1,0:T(8,128)(2,1)S(1)} %get-tuple-element.31), channel_id=1, source_target_pairs={{0,256},{256,0},{1,257},{257,1},{2,258},{258,2},{3,259},{259,3},{4... | collective-permute-start | bytes 3440648 | tf_op jit(solution)/shard_map/ppermute | solution.py:262
  72.4 17.2 %collective-permute-start = (f32[32,1024]{1,0:T(8,128)S(1)}, f32[32,1024]{1,0:T(8,128)S(1)}, u32[]{:S(2)}, u32[]{:S(2)}) collective-permute-start(f32[32,1024]{1,0:T(8,128)S(1)} %bitcast.87), channel_id=1, source_target_pairs={{0,256},{256,0},{1,257},{257,1},{2,258},{258,2},{3,259},{259,3},{4... | collective-permute-start | bytes 393224 | tf_op jit(solution)/shard_map/ppermute | solution.py:280
  91.9 1.3 copy-start.5
  100.7 1.1 copy-start.2
  101.7 45.2 %all-to-all-start.2 = ((bf16[64,80,128]{2,1,0:T(8,128)(2,1)}), bf16[64,80,128]{2,1,0:T(8,128)(2,1)S(1)}, u32[]{:S(2)}, u32[]{:S(2)}) async-start(bf16[64,80,128]{2,1,0:T(8,128)(2,1)} %bitcast.74), calls=%async_computation.2 | async-start | bytes 2621440 | tf_op jit(solution)/shard_map/all_to_all | solution.py:288
  112.7 18.5 %collective-permute-start.2 = (f32[32,1024]{1,0:T(8,128)S(1)}, f32[32,1024]{1,0:T(8,128)S(1)}, u32[]{:S(2)}, u32[]{:S(2)}) collective-permute-start(f32[32,1024]{1,0:T(8,128)S(1)} %get-tuple-element.35), channel_id=1, source_target_pairs={{0,256},{256,0},{1,257},{257,1},{2,258},{258,2},{3,259},{259,3},{4... | collective-permute-start | bytes 393224 | tf_op jit(solution)/shard_map/ppermute | solution.py:292
Sparse Core Ops, SparseCore 0:
  43.0 48.8 all-gather.3
  94.6 35.3 all-gather.5
